TPU v7x, 32 devices: a whole 2x2x4 slice. The times are simulated.
32 devices in a mesh: dp: 8 (over y, x, core), tensor: 4 (over z).
Axes of the slice: x: 2, y: 2, z: 4, core: 2. Of those that a mesh axis runs over, the one named last changes fastest.
Arguments:
- x_post: bfloat16 [1024, 32, 512], P('tensor', 'dp'), may hold values from -6 to 6
- x_dual: bfloat16 [1024, 32, 512], P('tensor', 'dp'), may hold values from -6 to 6
- cot_post: bfloat16 [1024, 32, 512], P('tensor', 'dp'), may hold values from -6 to 6
- cot_dual: bfloat16 [1024, 32, 512], P('tensor', 'dp'), may hold values from -6 to 6
- segment_ids: int32 [1024, 32], P(None, 'dp'), may hold values from 0 to 3, as said below
- w_qkv: bfloat16 [3, 512, 512], P(None, None, 'tensor'), may hold values from -0.375 to 0.375
- w_out: bfloat16 [512, 512], P('tensor'), may hold values from -0.5 to 0.5
- w_up: bfloat16 [512, 2048], P(None, 'tensor'), may hold values from -0.25 to 0.25
- w_down: bfloat16 [2048, 512], P('tensor'), may hold values from -0.125 to 0.125
- gain_one: float32 [512], replicated, may hold values from 0.1 to 1.9
- bias_one: float32 [512], replicated, may hold values from -4 to 4
- gain_two: float32 [512], replicated, may hold values from 0.1 to 1.9
- bias_two: float32 [512], replicated, may hold values from -4 to 4
Outputs:
- post_out: float32 [1024, 32, 512], P('tensor', 'dp')
- dual_out: float32 [1024, 32, 512], P('tensor', 'dp')
- grad_post: float32 [1024, 32, 512], P('tensor', 'dp')
- grad_qkv: float32 [3, 512, 512], P(None, 'dp', 'tensor')
- grad_out: float32 [512, 512], P('tensor', 'dp')
- grad_up: float32 [512, 2048], P('dp', 'tensor')
- grad_down: float32 [2048, 512], P('tensor', 'dp')
- grad_gain_one: float32 [512], P(('dp', 'tensor'))
- grad_bias_one: float32 [512], P(('dp', 'tensor'))
- grad_gain_two: float32 [512], P(('dp', 'tensor'))
- grad_bias_two: float32 [512], P(('dp', 'tensor'))
Inputs may be any that keep to these rules, and one draw needn't show every extreme that they name: `segment_ids`: down each column (one packed row of 1024 tokens) the ids start at 0 and never fall; equal ids mark one document. In each aligned block of 4 columns one column holds a single document; every other column holds exactly four documents.
All inputs are finite; a program needn't handle non-finite values.
Results may differ from a plain program's by a relative error of at most 0.017.
The roundings to bfloat16 on the way count: a program that leaves them out, or rounds other values in their place, can miss the bound.
Values may be sent and summed in bfloat16 or wider, within the bound.
A program may use at most 192 MiB of HBM per device.

v0:
```python
import jax
import jax.numpy as jnp
from jax import lax
from jax.sharding import PartitionSpec as P

E = 64


EPSILON = 1e-05


def layer_norm(total, gain, bias):
    centre = total - jnp.mean(total, axis=-1, keepdims=True)
    factor = lax.rsqrt(jnp.mean(centre * centre, axis=-1, keepdims=True) + EPSILON)
    normed = centre * factor
    return (normed * gain + bias, normed, factor)


def layer_norm_back(upstream, normed, factor, gain):
    scaled = upstream * gain
    inner = scaled - jnp.mean(scaled, axis=-1, keepdims=True)
    inner = inner - normed * jnp.mean(scaled * normed, axis=-1, keepdims=True)
    leading = tuple(range(upstream.ndim - 1))
    return (
        factor * inner,
        jnp.sum(upstream * normed, axis=leading),
        jnp.sum(upstream, axis=leading),
    )


def masked_scores(query_rows, key_rows, marks):
    scores = (
        jnp.einsum("qe,ke->qk", query_rows, key_rows, preferred_element_type=jnp.float32) * 0.125
    )
    return jnp.where(marks[:, None] == marks[None, :], scores, -1e30)


def attend(query, keys, values, labels):

    def single(item):
        query_rows, key_rows, value_rows, marks = item
        scores = masked_scores(query_rows, key_rows, marks)
        top = jnp.max(scores, axis=-1, keepdims=True)
        raised = jnp.exp(scores - top)
        denom = jnp.sum(raised, axis=-1, keepdims=True)
        probs = (raised / denom).astype(jnp.bfloat16)
        result = jnp.dot(probs, value_rows, preferred_element_type=jnp.float32).astype(jnp.bfloat16)
        return (result, (top + jnp.log(denom))[:, 0])

    return lax.map(single, (query, keys, values, labels))


def attend_back(query, keys, values, upstream, logsum, labels):

    def single(item):
        query_rows, key_rows, value_rows, up_rows, lse_rows, marks = item
        scores = masked_scores(query_rows, key_rows, marks)
        probs = jnp.exp(scores - lse_rows[:, None])
        pushed = jnp.einsum("qe,ke->qk", up_rows, value_rows, preferred_element_type=jnp.float32)
        delta = probs * (pushed - jnp.sum(probs * pushed, axis=-1, keepdims=True))
        low_delta = delta.astype(jnp.bfloat16)
        grad_query = (
            jnp.dot(low_delta, key_rows, preferred_element_type=jnp.float32) * 0.125
        ).astype(jnp.bfloat16)
        grad_keys = (
            jnp.einsum("qk,qe->ke", low_delta, query_rows, preferred_element_type=jnp.float32)
            * 0.125
        ).astype(jnp.bfloat16)
        grad_values = jnp.einsum(
            "qk,qe->ke", probs.astype(jnp.bfloat16), up_rows, preferred_element_type=jnp.float32
        ).astype(jnp.bfloat16)
        return (grad_query, grad_keys, grad_values)

    return lax.map(single, (query, keys, values, upstream, logsum, labels))


def run_layer(post, dual, cot_one, cot_two, labels, w_qkv, w_out, w_up, w_down, norms, moves):
    (
        gather_in,
        sum_attn,
        gather_mid,
        sum_ffn,
        gather_ffn_grad,
        sum_mid_grad,
        gather_attn_grad,
        sum_in_grad,
    ) = moves
    gain_one, bias_one, gain_two, bias_two = norms
    width = w_qkv.shape[1]
    local_width = w_qkv.shape[2]
    heads = local_width // E
    hidden_width = w_up.shape[1]
    own_rows = post.shape[0]
    joined = jnp.transpose(w_qkv, (1, 0, 2)).reshape(width, 3 * local_width)
    tokens = gather_in(post)
    length, columns = (tokens.shape[0], tokens.shape[1])
    flat_tokens = tokens.reshape(length * columns, width)
    projected = jnp.dot(flat_tokens, joined, preferred_element_type=jnp.float32).astype(
        jnp.bfloat16
    )
    split = projected.reshape(length, columns, 3, heads, E).transpose(2, 1, 3, 0, 4)
    split = split.reshape(3, columns * heads, length, E)
    marks = jnp.repeat(labels.T, heads, axis=0)
    attended, logsum = attend(split[0], split[1], split[2], marks)
    mixed = (
        attended.reshape(columns, heads, length, E)
        .transpose(2, 0, 1, 3)
        .reshape(length, columns, local_width)
    )

    def attn_term(start, count):
        return jnp.einsum("rbf,fd->rbd", mixed, w_out, preferred_element_type=jnp.float32)

    branch_one = sum_attn(attn_term, own_rows)
    middle, normed_one, factor_one = layer_norm(
        post.astype(jnp.float32) + branch_one, gain_one, bias_one
    )
    dual_mid = dual.astype(jnp.float32) + branch_one
    middle_all = gather_mid(middle.astype(jnp.bfloat16))
    mid_length = middle_all.shape[0]
    flat_middle = middle_all.reshape(mid_length * columns, width)
    inner = jnp.dot(flat_middle, w_up, preferred_element_type=jnp.float32)
    hidden = jax.nn.gelu(inner).astype(jnp.bfloat16)
    hidden_rows = hidden.reshape(mid_length, columns, hidden_width)

    def ffn_term(start, count):
        return jnp.einsum("rbf,fd->rbd", hidden_rows, w_down, preferred_element_type=jnp.float32)

    branch_two = sum_ffn(ffn_term, own_rows)
    post_out, normed_two, factor_two = layer_norm(middle + branch_two, gain_two, bias_two)
    dual_out = dual_mid + branch_two
    dual_grad = cot_two.astype(jnp.float32)
    d_two, grad_gain_two, grad_bias_two = layer_norm_back(
        cot_one.astype(jnp.float32), normed_two, factor_two, gain_two
    )
    up_two = gather_ffn_grad((d_two + dual_grad).astype(jnp.bfloat16))
    flat_up_two = up_two.reshape(mid_length * columns, width)
    grad_down = jnp.einsum("rf,rd->fd", hidden, flat_up_two, preferred_element_type=jnp.float32)
    hidden_grad = jnp.einsum("rd,fd->rf", flat_up_two, w_down, preferred_element_type=jnp.float32)
    _, gelu_back = jax.vjp(jax.nn.gelu, inner)
    grad_inner = gelu_back(hidden_grad)[0].astype(jnp.bfloat16)
    grad_up = jnp.einsum("rd,rf->df", flat_middle, grad_inner, preferred_element_type=jnp.float32)
    inner_rows = grad_inner.reshape(mid_length, columns, hidden_width)

    def mid_grad_term(start, count):
        return jnp.einsum("rbf,df->rbd", inner_rows, w_up, preferred_element_type=jnp.float32)

    grad_middle = d_two + sum_mid_grad(mid_grad_term, own_rows)
    d_one, grad_gain_one, grad_bias_one = layer_norm_back(
        grad_middle, normed_one, factor_one, gain_one
    )
    up_one = gather_attn_grad((d_one + dual_grad).astype(jnp.bfloat16))
    flat_up_one = up_one.reshape(length * columns, width)
    grad_out = jnp.einsum(
        "rf,rd->fd",
        mixed.reshape(length * columns, local_width),
        flat_up_one,
        preferred_element_type=jnp.float32,
    )
    grad_mixed = jnp.einsum(
        "rd,fd->rf", flat_up_one, w_out, preferred_element_type=jnp.float32
    ).astype(jnp.bfloat16)
    grad_mixed = (
        grad_mixed.reshape(length, columns, heads, E)
        .transpose(1, 2, 0, 3)
        .reshape(columns * heads, length, E)
    )
    grad_query, grad_keys, grad_values = attend_back(
        split[0], split[1], split[2], grad_mixed, logsum, marks
    )
    grad_proj = jnp.stack([grad_query, grad_keys, grad_values]).reshape(
        3, columns, heads, length, E
    )
    grad_proj = grad_proj.transpose(3, 1, 0, 2, 4).reshape(length * columns, 3 * local_width)
    grad_joined = jnp.einsum(
        "rd,rc->dc", flat_tokens, grad_proj, preferred_element_type=jnp.float32
    )
    grad_qkv = grad_joined.reshape(width, 3, local_width).transpose(1, 0, 2)
    proj_rows = grad_proj.reshape(length, columns, 3 * local_width)

    def input_grad_term(start, count):
        return jnp.einsum("rbc,dc->rbd", proj_rows, joined, preferred_element_type=jnp.float32)

    grad_post = d_one + sum_in_grad(input_grad_term, own_rows)
    norm_stack = jnp.stack([grad_gain_one, grad_bias_one, grad_gain_two, grad_bias_two])
    return (post_out, dual_out, grad_post, (grad_qkv, grad_out, grad_up, grad_down), norm_stack)


def body(
    x_post,
    x_dual,
    cot_post,
    cot_dual,
    segment_ids,
    w_qkv,
    w_out,
    w_up,
    w_down,
    gain_one,
    bias_one,
    gain_two,
    bias_two,
):
    norms = (gain_one, bias_one, gain_two, bias_two)
    gather_in = lambda array: lax.all_gather(array, "tensor", axis=0, tiled=True)
    sum_attn = lambda term_of, count: lax.psum_scatter(
        term_of(jnp.int32(0), count * lax.axis_size("tensor")),
        "tensor",
        scatter_dimension=0,
        tiled=True,
    )
    gather_attn_grad = lambda array: lax.all_gather(array, "tensor", axis=0, tiled=True)
    sum_in_grad = lambda term_of, count: lax.psum_scatter(
        term_of(jnp.int32(0), count * lax.axis_size("tensor")).astype(jnp.bfloat16),
        "tensor",
        scatter_dimension=0,
        tiled=True,
    ).astype(jnp.float32)
    moves = (
        gather_in,
        sum_attn,
        lambda array: lax.all_gather(array, "tensor", axis=0, tiled=True),
        lambda term_of, count: lax.psum_scatter(
            term_of(jnp.int32(0), count * lax.axis_size("tensor")),
            "tensor",
            scatter_dimension=0,
            tiled=True,
        ),
        lambda array: lax.all_gather(array, "tensor", axis=0, tiled=True),
        lambda term_of, count: lax.psum_scatter(
            term_of(jnp.int32(0), count * lax.axis_size("tensor")),
            "tensor",
            scatter_dimension=0,
            tiled=True,
        ),
        gather_attn_grad,
        sum_in_grad,
    )
    post_out, dual_out, grad_post, grads, norm_stack = run_layer(
        x_post, x_dual, cot_post, cot_dual, segment_ids, w_qkv, w_out, w_up, w_down, norms, moves
    )
    grad_qkv, grad_out, grad_up, grad_down = (
        lax.psum_scatter(
            grads[0].astype(jnp.bfloat16), "dp", scatter_dimension=1, tiled=True
        ).astype(jnp.float32),
        lax.psum_scatter(
            grads[1].astype(jnp.bfloat16), "dp", scatter_dimension=1, tiled=True
        ).astype(jnp.float32),
        lax.psum_scatter(
            grads[2].astype(jnp.bfloat16), "dp", scatter_dimension=0, tiled=True
        ).astype(jnp.float32),
        lax.psum_scatter(
            grads[3].astype(jnp.bfloat16), "dp", scatter_dimension=1, tiled=True
        ).astype(jnp.float32),
    )
    norm_parts = lax.psum_scatter(norm_stack, ("dp", "tensor"), scatter_dimension=1, tiled=True)
    return (
        post_out,
        dual_out,
        grad_post,
        grad_qkv,
        grad_out,
        grad_up,
        grad_down,
        norm_parts[0],
        norm_parts[1],
        norm_parts[2],
        norm_parts[3],
    )


def solution(mesh):
    placed = (
        P("tensor", "dp", None),
        P("tensor", "dp", None),
        P("tensor", "dp", None),
        P("tensor", "dp", None),
        P(None, "dp"),
        P(None, None, "tensor"),
        P("tensor", None),
        P(None, "tensor"),
        P("tensor", None),
        P(),
        P(),
        P(),
        P(),
    )
    return jax.shard_map(
        body,
        mesh=mesh,
        in_specs=placed,
        out_specs=(
            P("tensor", "dp", None),
            P("tensor", "dp", None),
            P("tensor", "dp", None),
            P(None, "dp", "tensor"),
            P("tensor", "dp"),
            P("dp", "tensor"),
            P("tensor", "dp"),
            P(("dp", "tensor")),
            P(("dp", "tensor")),
            P(("dp", "tensor")),
            P(("dp", "tensor")),
        ),
        check_vma=False,
    )
```

profile of v0, /device:TPU:0, one launch (start us, length us, event | category | flops | bytes accessed | tf_op | source)
XLA Modules:
  0.0 1326.3 jit_solution(3840806140461398813)
XLA Ops:
  9.9 83.2 %all-gather.5.cloned.1.call-done = bf16[1024,4,512]{2,1,0:T(4,128)(2,1)} async-done(((bf16[256,4,512]{2,1,0:T(4,128)(2,1)}), bf16[1024,4,512]{2,1,0:T(4,128)(2,1)}) %all-gather.5.cloned.1.call-update) | async-done | bytes 4194320 | tf_op jit(solution)/shard_map/all_gather | solution.py:205
  93.1 6.9 reshape.155
  100.0 6.3 convolution_convert_fusion
  106.3 11.8 reshape.157
  118.1 6.1 fusion.86
  128.9 46.4 %while.26 = (s32[]{:T(128)}, bf16[8,1024,64]{1,2,0:T(8,128)(2,1)}, f32[8,1024]{1,0:T(8,128)S(1)}, s32[8,1024]{1,0:T(8,128)S(1)}, bf16[8,1024,64]{2,1,0:T(8,128)(...) while((s32[]{:T(128)}, bf16[8,1024,64]{1,2,0:T(8,128)(2,1)}, ...), condition=%wide.region_3.4_spmd, body=%wide.region_0.3_spmd.sunk | while | flops 284228608 | bytes 13572205 | solution.py:50
  143.3 3.0 fusion.128
  172.3 3.0 fusion.128
  175.4 6.5 fusion.79
  182.2 142.9 %reduce-scatter.12.cloned.1.call-done = f32[256,4,512]{2,0,1:T(8,128)} async-done(((f32[1024,4,512]{2,0,1:T(8,128)}), f32[256,4,512]{2,0,1:T(8,128)}) %reduce-scatter.12.cloned.1.call-update) | async-done | bytes 2097168 | tf_op jit(solution)/shard_map/reduce_scatter | solution.py:206
  329.3 81.6 %all-gather.7.cloned.1.call-done = bf16[1024,4,512]{2,0,1:T(8,128)(2,1)} async-done(((bf16[256,4,512]{2,0,1:T(8,128)(2,1)}), bf16[1024,4,512]{2,0,1:T(8,128)(2,1)}) %all-gather.7.cloned.1.call-update) | async-done | bytes 4194320 | tf_op jit(solution)/shard_map/all_gather | solution.py:222
  410.9 7.3 copy.74
  418.2 6.9 reshape.160
  425.1 8.5 multiply_convert_fusion.1
  433.7 7.0 reshape.161
  440.7 7.8 fusion.63
  448.6 143.1 %reduce-scatter.14.cloned.1.call-done = f32[256,4,512]{2,0,1:T(8,128)} async-done(((f32[1024,4,512]{2,0,1:T(8,128)}), f32[256,4,512]{2,0,1:T(8,128)}) %reduce-scatter.14.cloned.1.call-update) | async-done | bytes 2097168 | tf_op jit(solution)/shard_map/reduce_scatter | solution.py:223
  591.6 4.8 fusion.83
  600.6 81.2 %all-gather.9.cloned.1.call-done = bf16[1024,4,512]{2,0,1:T(8,128)(2,1)} async-done(((bf16[256,4,512]{2,0,1:T(8,128)(2,1)}), bf16[1024,4,512]{2,0,1:T(8,128)(2,1)}) %all-gather.9.cloned.1.call-update) | async-done | bytes 4194320 | tf_op jit(solution)/shard_map/all_gather | solution.py:229
  681.8 7.4 copy.79
  689.1 6.9 reshape.162
  696.1 11.1 fusion.60
  707.1 6.9 reshape.163
  714.1 7.8 fusion.61
  722.0 143.1 %reduce-scatter.16.cloned.1.call-done = f32[256,4,512]{2,0,1:T(8,128)} async-done(((f32[1024,4,512]{2,0,1:T(8,128)}), f32[256,4,512]{2,0,1:T(8,128)}) %reduce-scatter.16.cloned.1.call-update) | async-done | bytes 2097168 | tf_op jit(solution)/shard_map/reduce_scatter | solution.py:230
  865.1 4.8 multiply_reduce_fusion.1
  874.1 6.6 convolution_convert_fusion.3
  880.8 7.3 convolution_convert_fusion.4
  888.2 6.0 copy.90
  894.2 4.8 reshape_reshape.7
  899.9 55.6 %all-gather.11.cloned.1.call-done = bf16[1024,4,512]{2,0,1:T(8,128)(2,1)} async-done(((bf16[256,4,512]{2,0,1:T(8,128)(2,1)}), bf16[1024,4,512]{2,0,1:T(8,128)(2,1)}) %all-gather.11.cloned.1.call-update) | async-done | bytes 4194320 | tf_op jit(solution)/shard_map/all_gather | solution.py:212
  955.5 7.3 copy.81
  962.9 7.2 reshape.164
  970.1 4.6 convolution_convert_fusion.1
  977.1 5.0 reshape.165
  982.1 3.2 copy.84
  988.6 99.4 %while.27 = (s32[]{:T(128)}, bf16[8,1024,64]{1,2,0:T(8,128)(2,1)}, bf16[8,1024,64]{1,2,0:T(8,128)(2,1)}, bf16[8,1024,64]{1,2,0:T(8,128)(2,1)}, s32[8,1024]{1,0:T...) while((s32[]{:T(128)}, bf16[8,1024,64]{1,2,0:T(8,128)(2,1)}, ...), condition=%wide.region_17.18_spmd, body=%wide.region_15.17_spmd.sunk | while | flops 681901056 | bytes 33727612 | solution.py:74
  1088.0 4.2 fusion.81
  1092.2 15.8 %copy.88 = bf16[1024,4,3,2,64]{4,3,2,1,0:T(2,128)(2,1)} copy(bf16[1024,4,3,2,64]{0,4,3,2,1:T(8,128)(2,1)} %get-tuple-element.229) | data formatting | bytes 6291456 | tf_op jit(solution)/shard_map/transpose | solution.py:174
  1108.1 11.7 reshape.167
  1120.1 5.0 convolution_convert_fusion.5
  1126.1 6.2 convolution_convert_fusion.2
  1132.3 4.3 copy.92
  1139.6 4.3 copy.91
  1143.9 21.0 %reduce-scatter.28.cloned.1.call-done = f32[16,4]{1,0:T(8,128)} async-done(((f32[512,4]{1,0:T(8,128)}), f32[16,4]{1,0:T(8,128)}) %reduce-scatter.28.cloned.1.call-update) | async-done | bytes 272
  1168.1 29.7 %reduce-scatter.22.cloned.1.call-done = bf16[128,64]{0,1:T(8,128)(2,1)} async-done(((bf16[128,512]{0,1:T(8,128)(2,1)}), bf16[128,64]{0,1:T(8,128)(2,1)}) %reduce-scatter.22.cloned.1.call-update) | async-done | bytes 16400 | tf_op jit(solution)/shard_map/reduce_scatter | solution.py:246
  1199.1 36.0 %reduce-scatter.20.cloned.1.call-done = bf16[3,64,128]{2,1,0:T(8,128)(2,1)} async-done(((bf16[3,512,128]{2,1,0:T(8,128)(2,1)}), bf16[3,64,128]{2,1,0:T(8,128)(2,1)}) %reduce-scatter.20.cloned.1.call-update) | async-done | bytes 49168 | tf_op jit(solution)/shard_map/reduce_scatter | solution.py:243
  1236.6 77.6 %reduce-scatter.18.cloned.1.call-done = bf16[256,4,512]{2,0,1:T(8,128)(2,1)} async-done(((bf16[1024,4,512]{2,0,1:T(8,128)(2,1)}), bf16[256,4,512]{2,0,1:T(8,128)(2,1)}) %reduce-scatter.18.cloned.1.call-update) | async-done | bytes 1048592 | tf_op jit(solution)/shard_map/reduce_scatter | solution.py:213
  (212 shorter events, 181.9 us)
Async XLA Ops:
  7.2 418.0 %copy-start = (bf16[512,512]{1,0:T(8,128)(2,1)S(1)}, bf16[512,512]{1,0:T(8,128)(2,1)}, u32[]{:S(2)}) copy-start(bf16[512,512]{1,0:T(8,128)(2,1)} %param.24) | copy-start | bytes 1572868
  7.2 85.9 %all-gather.5.cloned.1.call-start = ((), (), s32[]{:S(2)}) async-start(), calls=%async_computation.9 | async-start | bytes 5242880 | tf_op jit(solution)/shard_map/all_gather | solution.py:205
  7.9 317.1 %reduce-scatter.12.cloned.1.call-start = ((), (), s32[]{:S(2)}) async-start(), calls=%async_computation.10 | async-start | bytes 10485760 | tf_op jit(solution)/shard_map/reduce_scatter | solution.py:206
  9.9 90.1 %copy-start.11 = (bf16[3,512,128]{1,2,0:T(8,128)(2,1)}, bf16[3,512,128]{1,2,0:T(8,128)(2,1)S(1)}, u32[]{:S(2)}) copy-start(bf16[3,512,128]{1,2,0:T(8,128)(2,1)S(1)} %copy.69) | copy-start | bytes 1179652
  128.9 46.4 %copy-start.9 = (bf16[128,512]{1,0:T(8,128)(2,1)S(1)}, bf16[128,512]{1,0:T(8,128)(2,1)}, u32[]{:S(2)}) copy-start(bf16[128,512]{1,0:T(8,128)(2,1)} %param.23) | copy-start | bytes 393220
  175.3 6.5 copy-start.5
  181.9 145.9 %copy-start.13 = (f32[512]{0:T(512)S(1)}, f32[512]{0:T(512)}, u32[]{:S(2)}) copy-start(f32[512]{0:T(512)} %param.26) | copy-start | bytes 6148
  181.9 145.9 %copy-start.15 = (f32[512]{0:T(512)S(1)}, f32[512]{0:T(512)}, u32[]{:S(2)}) copy-start(f32[512]{0:T(512)} %param.27) | copy-start | bytes 6148
  181.9 229.0 %all-gather.7.cloned.1.call-start = ((), (), s32[]{:S(2)}) async-start(), calls=%async_computation.11 | async-start | bytes 5242880 | tf_op jit(solution)/shard_map/all_gather | solution.py:222
  329.2 262.4 %reduce-scatter.14.cloned.1.call-start = ((), (), s32[]{:S(2)}) async-start(), calls=%async_computation.12 | async-start | bytes 10485760 | tf_op jit(solution)/shard_map/reduce_scatter | solution.py:223
  433.7 7.0 copy-start.10
  448.5 148.4 %copy-start.14 = (f32[512]{0:T(512)S(1)}, f32[512]{0:T(512)}, u32[]{:S(2)}) copy-start(f32[512]{0:T(512)} %param.28) | copy-start | bytes 6148
  448.5 233.2 %all-gather.9.cloned.1.call-start = ((), (), s32[]{:S(2)}) async-start(), calls=%async_computation.13 | async-start | bytes 5242880 | tf_op jit(solution)/shard_map/all_gather | solution.py:229
  591.6 5.3 copy-start.6
  596.5 1.6 copy-start.2
  596.5 2.0 copy-start.7
  600.1 265.0 %reduce-scatter.16.cloned.1.call-start = ((), (), s32[]{:S(2)}) async-start(), calls=%async_computation.14 | async-start | bytes 10485760 | tf_op jit(solution)/shard_map/reduce_scatter | solution.py:230
  721.9 143.2 %copy-start.16 = (f32[512]{0:T(512)S(1)}, f32[512]{0:T(512)}, u32[]{:S(2)}) copy-start(f32[512]{0:T(512)} %param.29) | copy-start | bytes 6148
  721.9 233.6 %all-gather.11.cloned.1.call-start = ((), (), s32[]{:S(2)}) async-start(), calls=%async_computation.15 | async-start | bytes 5242880 | tf_op jit(solution)/shard_map/all_gather | solution.py:212
  869.8 1.4 copy-start.4
  873.9 262.7 %reduce-scatter.26.cloned.1.call-start = ((), (), s32[]{:S(2)}) async-start(), calls=%async_computation.20 | async-start | bytes 589824 | tf_op jit(solution)/shard_map/reduce_scatter | solution.py:252
  880.8 257.3 %reduce-scatter.24.cloned.1.call-start = ((), (), s32[]{:S(2)}) async-start(), calls=%async_computation.19 | async-start | bytes 589824 | tf_op jit(solution)/shard_map/reduce_scatter | solution.py:249
  888.2 276.7 %reduce-scatter.28.cloned.1.call-start = ((), (), s32[]{:S(2)}) async-start(), calls=%async_computation.21 | async-start | bytes 270336
  899.9 297.9 %reduce-scatter.22.cloned.1.call-start = ((), (), s32[]{:S(2)}) async-start(), calls=%async_computation.18 | async-start | bytes 147456 | tf_op jit(solution)/shard_map/reduce_scatter | solution.py:246
  970.1 4.6 copy-start.3
  970.1 4.6 copy-start.8
  1119.8 6.3 copy-start.12
  1119.8 115.4 %reduce-scatter.20.cloned.1.call-start = ((), (), s32[]{:S(2)}) async-start(), calls=%async_computation.17 | async-start | bytes 442368 | tf_op jit(solution)/shard_map/reduce_scatter | solution.py:243
  1126.0 188.3 %reduce-scatter.18.cloned.1.call-start = ((), (), s32[]{:S(2)}) async-start(), calls=%async_computation.16 | async-start | bytes 5242880 | tf_op jit(solution)/shard_map/reduce_scatter | solution.py:213
  1314.3 5.0 copy-start.1
Sparse Core Ops, SparseCore 0:
  9.6 83.4 all-gather.4
  182.0 142.9 reduce-scatter.11
  329.3 81.4 all-gather.6
  448.6 142.9 reduce-scatter.13
  600.2 81.4 all-gather.8
  722.0 142.9 reduce-scatter.15
  874.0 81.4 all-gather.10
  958.6 32.6 reduce-scatter.25
  994.7 34.1 reduce-scatter.23
  1031.0 133.8 reduce-scatter.27
  1168.1 29.6 reduce-scatter.21
  1201.3 33.8 reduce-scatter.19
  1237.5 76.7 reduce-scatter.17
where the time goes:
time: 1340 us; the launch traced here: 1330 us
  waiting for transfers between devices  896 us (67%)
  matrix products  207 us (15%)
  local copies, waits for them, and re-layouts  157 us (12%)
  other arithmetic  49.4 us (4%)
  between operations  14.6 us (1%)
    reduce_scatter x3, waiting for transfers between devices, body(): lax.psum_scatter(term_of(jnp.int32(0), count * lax.axis_size('tensor')),...  429 us
    all_gather x4, waiting for transfers between devices, body(): lax.all_gather(array, 'tensor', axis=0, tiled=True)  302 us
    reduce_scatter x1, waiting for transfers between devices, body(): lax.psum_scatter(term_of(jnp.int32(0), count * lax.axis_size('tensor')).a...  77.6 us
    reduce_scatter x1, waiting for transfers between devices, body(): lax.psum_scatter(grads[0].astype(jnp.bfloat16), 'dp', scatter_dimension=1...  36 us
    dot_general x16, matrix products, masked_scores(): jnp.einsum('qe,ke->qk', query_rows, key_rows, preferred_element_type=jnp....  34.4 us
    reduce_scatter x1, waiting for transfers between devices, body(): lax.psum_scatter(grads[1].astype(jnp.bfloat16), 'dp', scatter_dimension=1...  29.7 us
  transfers between devices with their start and end apart: 13, of which 11 were waited for; matrix products, arithmetic and copies ran while one was open for 17% of the time, Pallas kernels for 0%

commit v1 on v0

v1 whole, which is shorter than its diff:
```python
import functools

import jax
import jax.numpy as jnp
from jax import lax
from jax.experimental import pallas as pl
from jax.experimental.pallas import tpu as pltpu
from jax.sharding import PartitionSpec as P

E = 64
EPSILON = 1e-05
NEGATIVE = -1e30
GELU_A = 0.7978845608028654
GELU_B = 0.044715
F32 = jnp.float32
BF16 = jnp.bfloat16
VMEM_BYTES = 60 * 1024 * 1024


def dot_nn(a, b):
    return lax.dot_general(a, b, (((1,), (0,)), ((), ())), preferred_element_type=F32)


def dot_nt(a, b):
    return lax.dot_general(a, b, (((1,), (1,)), ((), ())), preferred_element_type=F32)


def dot_tn(a, b):
    return lax.dot_general(a, b, (((0,), (0,)), ((), ())), preferred_element_type=F32)


def row_mean(a):
    return jnp.mean(a, axis=-1, keepdims=True)


def norm_forward(total):
    centre = total - row_mean(total)
    factor = lax.rsqrt(row_mean(centre * centre) + EPSILON)
    return centre * factor, factor


def norm_backward(upstream, normed, factor, gain):
    scaled = upstream * gain
    inner = scaled - row_mean(scaled) - normed * row_mean(scaled * normed)
    return factor * inner


def mask_bias(seg_keys, seg_own, column, bias_ref):
    lanes = lax.broadcasted_iota(jnp.int32, seg_keys.shape, 1)
    keys = jnp.sum(jnp.where(lanes == column, seg_keys, 0.0), axis=1, keepdims=True)
    bias_ref[...] = jnp.where(keys == seg_own, 0.0, NEGATIVE)


def half_rows(block, half):
    zeros = jnp.zeros((E, block.shape[1]), block.dtype)
    if half == 0:
        return jnp.concatenate([block[:E], zeros], axis=0)
    return jnp.concatenate([zeros, block[E:]], axis=0)


def forward_kernel(
    seg_ref,
    seg_own_ref,
    x_all_ref,
    x_own_ref,
    dual_in_ref,
    cot_post_ref,
    cot_dual_ref,
    w_qkv_ref,
    w_out_ref,
    w_up_ref,
    w_down_ref,
    norms_ref,
    post_ref,
    dual_ref,
    d_one_ref,
    q_ref,
    k_ref,
    v_ref,
    do_ref,
    lse_ref,
    delta_ref,
    g_down_ref,
    g_up_ref,
    g_out_ref,
    g_norm_ref,
    bias_ref,
    qt_ref,
    vt_ref,
    ot_ref,
    hidden_ref,
    slope_ref,
    grad_inner_ref,
    up_two_ref,
    middle_ref,
    up_one_ref,
    mixed_ref,
):
    tensors, columns, rows, width = x_all_ref.shape
    length = tensors * rows
    heads = width // E
    pairs = heads // 2
    gain_one, bias_one = norms_ref[0:1, :], norms_ref[1:2, :]
    gain_two, bias_two = norms_ref[2:3, :], norms_ref[3:4, :]
    g_norm_ref[...] = jnp.zeros_like(g_norm_ref)

    @pl.loop(0, columns)
    def _(c):
        mask_bias(seg_ref[...], seg_own_ref[pl.ds(c, 1), :], c, bias_ref)
        x_own = x_own_ref[c]
        query = dot_nn(x_own, w_qkv_ref[0]).astype(BF16) * jnp.bfloat16(0.125)
        q_ref[c] = query
        qt_ref[...] = query.astype(F32).T.astype(BF16)

        @pl.loop(0, tensors)
        def _(t):
            block = x_all_ref[t, c]
            at = pl.ds(pl.multiple_of(t * rows, rows), rows)
            k_ref[c, at, :] = dot_nn(block, w_qkv_ref[1]).astype(BF16)
            v_ref[c, at, :] = dot_nn(block, w_qkv_ref[2]).astype(BF16)

        vt_ref[...] = v_ref[c].T

        @pl.loop(0, pairs)
        def _(j):
            at = pl.ds(pl.multiple_of(j * 2 * E, 2 * E), 2 * E)
            keys = k_ref[c, :, at]
            queries = qt_ref[at, :]
            for half in range(2):
                scores = dot_nn(keys, half_rows(queries, half)) + bias_ref[...]
                top = jnp.max(scores, axis=0, keepdims=True)
                raised = jnp.exp(scores - top)
                denom = jnp.sum(raised, axis=0, keepdims=True)
                at_head = pl.ds(pl.multiple_of((2 * j + half) * E, E), E)
                result = dot_nn(vt_ref[at_head, :], raised.astype(BF16))
                ot_ref[at_head, :] = result * (1.0 / denom)
                lse_ref[c, pl.ds(2 * j + half, 1), :] = top + jnp.log(denom)

        tokens = pl.ds(pl.multiple_of(c * rows, rows), rows)
        mixed = ot_ref[...].T.astype(BF16)
        mixed_ref[tokens, :] = mixed
        branch_one = dot_nn(mixed, w_out_ref[...])
        normed_one, factor_one = norm_forward(x_own.astype(F32) + branch_one)
        middle = normed_one * gain_one + bias_one
        middle_low = middle.astype(BF16)
        middle_ref[tokens, :] = middle_low
        branch_two = jnp.zeros((rows, width), F32)
        for t in range(tensors):
            inner = dot_nn(middle_low, w_up_ref[t])
            square = inner * inner
            bend = jnp.tanh(GELU_A * (inner + GELU_B * (square * inner)))
            hidden = (0.5 * inner * (1.0 + bend)).astype(BF16)
            slope_ref[t] = 0.5 * (1.0 + bend) + (0.5 * GELU_A) * inner * (1.0 - bend * bend) * (
                1.0 + (3.0 * GELU_B) * square
            )
            hidden_ref[t, tokens, :] = hidden
            branch_two = branch_two + dot_nn(hidden, w_down_ref[t])
        normed_two, factor_two = norm_forward(middle + branch_two)
        post_ref[c] = normed_two * gain_two + bias_two
        dual_ref[c] = dual_in_ref[c].astype(F32) + branch_one + branch_two
        cot_dual = cot_dual_ref[c].astype(F32)
        upstream = cot_post_ref[c].astype(F32)
        d_two = norm_backward(upstream, normed_two, factor_two, gain_two)
        g_norm_ref[2:3, :] += jnp.sum(upstream * normed_two, axis=0, keepdims=True)
        g_norm_ref[3:4, :] += jnp.sum(upstream, axis=0, keepdims=True)
        up_two = (d_two + cot_dual).astype(BF16)
        up_two_ref[tokens, :] = up_two
        grad_middle = d_two
        for t in range(tensors):
            grad_hidden = dot_nt(up_two, w_down_ref[t])
            grad_inner = (grad_hidden * slope_ref[t]).astype(BF16)
            grad_inner_ref[t, tokens, :] = grad_inner
            grad_middle = grad_middle + dot_nt(grad_inner, w_up_ref[t])
        d_one = norm_backward(grad_middle, normed_one, factor_one, gain_one)
        g_norm_ref[0:1, :] += jnp.sum(grad_middle * normed_one, axis=0, keepdims=True)
        g_norm_ref[1:2, :] += jnp.sum(grad_middle, axis=0, keepdims=True)
        d_one_ref[c] = d_one
        up_one = (d_one + cot_dual).astype(BF16)
        up_one_ref[tokens, :] = up_one
        grad_mixed = dot_nt(up_one, w_out_ref[...]).astype(BF16)
        do_ref[c] = grad_mixed
        product = grad_mixed.astype(F32).T * ot_ref[...]
        delta_ref[c] = jnp.sum(product.reshape(heads, E, rows), axis=1)

    @pl.loop(0, tensors)
    def _(t):
        g_down_ref[t] = dot_tn(up_two_ref[...], hidden_ref[t]).astype(BF16)
        g_up_ref[t] = dot_tn(middle_ref[...], grad_inner_ref[t]).astype(BF16)

    g_out_ref[...] = dot_tn(up_one_ref[...], mixed_ref[...]).astype(BF16)


def backward_kernel(
    seg_ref,
    seg_own_ref,
    x_all_ref,
    x_own_ref,
    w_qkv_ref,
    d_one_ref,
    q_ref,
    k_ref,
    v_ref,
    do_ref,
    lse_ref,
    delta_ref,
    base_ref,
    part_ref,
    g_qkv_ref,
    bias_ref,
    qt_ref,
    dot_ref,
    kt_ref,
    dk_ref,
    dv_ref,
    dqt_ref,
    acc_ref,
):
    tensors, columns, rows, width = x_all_ref.shape
    heads = width // E
    pairs = heads // 2
    acc_ref[...] = jnp.zeros_like(acc_ref)

    @pl.loop(0, columns)
    def _(c):
        mask_bias(seg_ref[...], seg_own_ref[pl.ds(c, 1), :], c, bias_ref)
        qt_ref[...] = q_ref[c].T
        dot_ref[...] = do_ref[c].T
        kt_ref[...] = k_ref[c].T

        @pl.loop(0, pairs)
        def _(j):
            at = pl.ds(pl.multiple_of(j * 2 * E, 2 * E), 2 * E)
            keys, values = k_ref[c, :, at], v_ref[c, :, at]
            queries, ups = q_ref[c, :, at], do_ref[c, :, at]
            sums = []
            for half in range(2):
                scores = dot_nn(keys, half_rows(qt_ref[at, :], half)) + bias_ref[...]
                probs = jnp.exp(scores - lse_ref[c, pl.ds(2 * j + half, 1), :])
                pushed = dot_nn(values, half_rows(dot_ref[at, :], half))
                delta = (probs * (pushed - delta_ref[c, pl.ds(2 * j + half, 1), :])).astype(BF16)
                at_head = pl.ds(pl.multiple_of((2 * j + half) * E, E), E)
                dqt_ref[at_head, :] = dot_nn(kt_ref[at_head, :], delta)
                sums.append((dot_nn(delta, queries), dot_nn(probs.astype(BF16), ups)))
            low_half = lax.broadcasted_iota(jnp.int32, sums[0][0].shape, 1) < E
            dk_ref[:, at] = jnp.where(low_half, sums[0][0], sums[1][0]).astype(BF16)
            dv_ref[:, at] = jnp.where(low_half, sums[0][1], sums[1][1]).astype(BF16)

        grad_query = (dqt_ref[...] * 0.125).T.astype(BF16)
        base_ref[c] = d_one_ref[c] + dot_nt(grad_query, w_qkv_ref[0])
        acc_ref[0] += dot_tn(x_own_ref[c], grad_query)

        @pl.loop(0, tensors)
        def _(t):
            at = pl.ds(pl.multiple_of(t * rows, rows), rows)
            grad_keys, grad_values = dk_ref[at, :], dv_ref[at, :]
            part = dot_nt(grad_keys, w_qkv_ref[1]) + dot_nt(grad_values, w_qkv_ref[2])
            part_ref[t, c] = part.astype(BF16)
            block = x_all_ref[t, c]
            acc_ref[1] += dot_tn(block, grad_keys)
            acc_ref[2] += dot_tn(block, grad_values)

    for i in range(3):
        g_qkv_ref[i] = acc_ref[i].astype(BF16)


def body(
    x_post,
    x_dual,
    cot_post,
    cot_dual,
    segment_ids,
    w_qkv,
    w_out,
    w_up,
    w_down,
    gain_one,
    bias_one,
    gain_two,
    bias_two,
):
    tensors = lax.axis_size("tensor")
    rows, columns, width = x_post.shape
    length = tensors * rows
    heads = width // E
    share = w_up.shape[1]
    me = lax.axis_index("tensor")
    x_own = jnp.swapaxes(x_post, 0, 1)
    x_all = lax.all_gather(x_own, "tensor", axis=0)
    all_qkv = lax.all_gather(w_qkv, "tensor", axis=2, tiled=True)
    all_out = lax.all_gather(w_out, "tensor", axis=0, tiled=True)
    all_up = lax.all_gather(w_up, "tensor", axis=0)
    all_down = lax.all_gather(w_down, "tensor", axis=0)
    norms = jnp.stack([gain_one, bias_one, gain_two, bias_two])
    seg = segment_ids.astype(F32)
    seg_own = lax.dynamic_slice_in_dim(seg.T, me * rows, rows, axis=1)
    in_vmem = pl.BlockSpec(memory_space=pltpu.VMEM)
    params = pltpu.CompilerParams(vmem_limit_bytes=VMEM_BYTES)
    shape = jax.ShapeDtypeStruct
    tokens = columns * rows
    forward = pl.pallas_call(
        forward_kernel,
        out_shape=(
            shape((columns, rows, width), F32),
            shape((columns, rows, width), F32),
            shape((columns, rows, width), F32),
            shape((columns, rows, width), BF16),
            shape((columns, length, width), BF16),
            shape((columns, length, width), BF16),
            shape((columns, rows, width), BF16),
            shape((columns, heads, rows), F32),
            shape((columns, heads, rows), F32),
            shape((tensors, width, share), BF16),
            shape((tensors, width, share), BF16),
            shape((width, width), BF16),
            shape((4, width), F32),
        ),
        in_specs=[in_vmem] * 12,
        out_specs=(in_vmem,) * 13,
        scratch_shapes=[
            pltpu.VMEM((length, rows), F32),
            pltpu.VMEM((width, rows), BF16),
            pltpu.VMEM((width, length), BF16),
            pltpu.VMEM((width, rows), F32),
            pltpu.VMEM((tensors, tokens, share), BF16),
            pltpu.VMEM((tensors, rows, share), F32),
            pltpu.VMEM((tensors, tokens, share), BF16),
            pltpu.VMEM((tokens, width), BF16),
            pltpu.VMEM((tokens, width), BF16),
            pltpu.VMEM((tokens, width), BF16),
            pltpu.VMEM((tokens, width), BF16),
        ],
        compiler_params=params,
        name="forward",
    )
    (
        post_out,
        dual_out,
        d_one,
        query,
        keys,
        values,
        grad_mixed,
        lse,
        delta,
        g_down,
        g_up,
        g_out,
        g_norm,
    ) = forward(
        seg, seg_own, x_all, x_own,
        jnp.swapaxes(x_dual, 0, 1), jnp.swapaxes(cot_post, 0, 1), jnp.swapaxes(cot_dual, 0, 1),
        all_qkv, all_out, all_up, all_down, norms,
    )
    backward = pl.pallas_call(
        backward_kernel,
        out_shape=(
            shape((columns, rows, width), F32),
            shape((tensors, columns, rows, width), BF16),
            shape((3, width, width), BF16),
        ),
        in_specs=[in_vmem] * 12,
        out_specs=(in_vmem,) * 3,
        scratch_shapes=[
            pltpu.VMEM((length, rows), F32),
            pltpu.VMEM((width, rows), BF16),
            pltpu.VMEM((width, rows), BF16),
            pltpu.VMEM((width, length), BF16),
            pltpu.VMEM((length, width), BF16),
            pltpu.VMEM((length, width), BF16),
            pltpu.VMEM((width, rows), F32),
            pltpu.VMEM((3, width, width), F32),
        ],
        compiler_params=params,
        name="backward",
    )
    base, part, g_qkv = backward(
        seg, seg_own, x_all, x_own, all_qkv, d_one, query, keys, values, grad_mixed, lse, delta
    )
    grad_post = base + lax.psum_scatter(part, "tensor", scatter_dimension=0, tiled=False).astype(F32)

    def over_dp(array, dim):
        return lax.psum_scatter(array, "dp", scatter_dimension=dim, tiled=True)

    own = width // tensors
    r_qkv = lax.psum_scatter(over_dp(g_qkv, 1), "tensor", scatter_dimension=2, tiled=True)
    r_out = lax.psum_scatter(over_dp(g_out, 0), "tensor", scatter_dimension=1, tiled=True)
    r_up = lax.psum_scatter(over_dp(g_up, 1), "tensor", scatter_dimension=0, tiled=False)
    r_down = lax.psum_scatter(over_dp(g_down, 1), "tensor", scatter_dimension=0, tiled=False)
    norm_parts = lax.psum_scatter(g_norm, ("dp", "tensor"), scatter_dimension=1, tiled=True)
    return (
        jnp.swapaxes(post_out, 0, 1),
        jnp.swapaxes(dual_out, 0, 1),
        jnp.swapaxes(grad_post, 0, 1),
        r_qkv.astype(F32),
        r_out.astype(F32).T,
        r_up.astype(F32),
        r_down.astype(F32).T,
        norm_parts[0],
        norm_parts[1],
        norm_parts[2],
        norm_parts[3],
    )


def solution(mesh):
    placed = (
        P("tensor", "dp", None),
        P("tensor", "dp", None),
        P("tensor", "dp", None),
        P("tensor", "dp", None),
        P(None, "dp"),
        P(None, None, "tensor"),
        P("tensor", None),
        P(None, "tensor"),
        P("tensor", None),
        P(),
        P(),
        P(),
        P(),
    )
    return jax.shard_map(
        body,
        mesh=mesh,
        in_specs=placed,
        out_specs=(
            P("tensor", "dp", None),
            P("tensor", "dp", None),
            P("tensor", "dp", None),
            P(None, "dp", "tensor"),
            P("tensor", "dp"),
            P("dp", "tensor"),
            P("tensor", "dp"),
            P(("dp", "tensor")),
            P(("dp", "tensor")),
            P(("dp", "tensor")),
            P(("dp", "tensor")),
        ),
        check_vma=False,
    )
```

time: 1340 us -> 782 us (0.58)
  waiting for transfers between devices: 896 us -> 590 us
  matrix products: 207 us -> 0 us
  local copies, waits for them, and re-layouts: 157 us -> 24.8 us
  Pallas kernels: 0 us -> 121 us
  other arithmetic: 49.4 us -> 6.45 us
  blocking collectives: 0 us -> 24.4 us
    reduce_scatter x8 -> x7, waiting for transfers between devices: 572 us -> 233 us  [the longest x4 120 us: over_dp(): return lax.psum_scatter(array, 'dp', scatter_dimension=dim, tiled=True)]
    dot_general x68 -> x0, matrix products: 207 us -> none  [the longest x16 34.4 us: masked_scores(): jnp.einsum('qe,ke->qk', query_rows, key_rows, preferred_element_type=jnp....]
    unnamed x14 -> x17, waiting for transfers between devices: 21.8 us -> 167 us
    pallas_call x0 -> x2, Pallas kernels: none -> 121 us  [the longest x1 69.1 us: body(): forward(seg, seg_own, x_all, x_own, jnp.swapaxes(x_dual, 0, 1), jnp.swapa...]
    all_gather x4, waiting for transfers between devices: 302 us -> 190 us  [the longest x1 80.9 us: body(): x_all = lax.all_gather(x_own, 'tensor', axis=0)]
    reshape x10 -> x0, local copies, waits for them, and re-layouts: 70.3 us -> none  [the longest x1 11.8 us: run_layer(): projected.reshape(length, columns, 3, heads, E).transpose(2, 1, 3, 0, 4)]
    all_gather x0 -> x1, blocking collectives: none -> 24.4 us  [body(): all_out = lax.all_gather(w_out, 'tensor', axis=0, tiled=True)]
    reduce_sum x14 -> x0, other arithmetic: 22.2 us -> none  [the longest x8 8.22 us: single(): denom = jnp.sum(raised, axis=-1, keepdims=True)]
  transfers between devices with their start and end apart: 13 -> 14, of which waited for: 11 -> 13; matrix products, arithmetic and copies ran while one was open for 17% -> 3% of each run, Pallas kernels for 0% -> 7%
where the time goes in v1:
time: 782 us; the launch traced here: 781 us
  waiting for transfers between devices  590 us (75%)
  Pallas kernels  121 us (15%)
  local copies, waits for them, and re-layouts  24.8 us (3%)
  blocking collectives  24.4 us (3%)
  between operations  14.1 us (2%)
    unnamed x17, waiting for transfers between devices  167 us
    reduce_scatter x4, waiting for transfers between devices, over_dp(): return lax.psum_scatter(array, 'dp', scatter_dimension=dim, tiled=True)  120 us
    all_gather x1, waiting for transfers between devices, body(): x_all = lax.all_gather(x_own, 'tensor', axis=0)  80.9 us
    reduce_scatter x1, waiting for transfers between devices, body(): lax.psum_scatter(part, 'tensor', scatter_dimension=0, tiled=False)  75.6 us
    pallas_call x1, Pallas kernels, body(): forward(seg, seg_own, x_all, x_own, jnp.swapaxes(x_dual, 0, 1), jnp.swapa...  69.1 us
    pallas_call x1, Pallas kernels, body(): backward(seg, seg_own, x_all, x_own, all_qkv, d_one, query, keys, values,...  52.1 us
    all_gather x1, waiting for transfers between devices, body(): all_up = lax.all_gather(w_up, 'tensor', axis=0)  47.7 us
    all_gather x1, waiting for transfers between devices, body(): all_down = lax.all_gather(w_down, 'tensor', axis=0)  46.3 us
  transfers between devices with their start and end apart: 14, of which 13 were waited for; matrix products, arithmetic and copies ran while one was open for 3% of the time, Pallas kernels for 7%

profile of v1, /device:TPU:0, one launch (start us, length us, event | category | flops | bytes accessed | tf_op | source)
XLA Modules:
  0.0 781.4 jit_solution(4301680230294890683)
XLA Ops:
  7.2 0.7 all-gather.8.cloned.1.call-update
  8.0 0.7 all-gather.12.cloned.1.call-update
  8.7 0.7 all-gather.14.cloned.1.call-update
  9.5 1.2 copy.57
  10.8 1.0 copy.37.seg_ref
  11.9 1.3 copy.56
  13.1 0.6 dynamic-slice_bitcast_fusion.seg_own_ref
  13.7 0.6 pad_maximum_fusion.norms_ref
  14.3 24.4 %all_gather.27.w_out_ref = bf16[512,512]{1,0:T(8,128)(2,1)} all-gather(bf16[128,512]{1,0:T(8,128)(2,1)S(1)} %copy-done.7), channel_id=1, replica_groups=mesh['dp'=8,'tensor'=4] {'tensor'}, dimensions={0}, use_global_device_ids=true | all-gather | bytes 655360 | tf_op jit(solution)/shard_map/all_gather | solution.py:290
  38.8 1.7 copy_bitcast_fusion
  40.5 15.2 %all-gather.8.cloned.1.call-done.w_qkv_ref = bf16[3,512,512]{2,1,0:T(8,128)(2,1)} async-done(((bf16[3,512,128]{2,1,0:T(8,128)(2,1)}), bf16[3,512,512]{2,1,0:T(8,128)(2,1)}) %all-gather.8.cloned.1.call-update) | async-done | bytes 1572880 | tf_op jit(solution)/shard_map/all_gather | solution.py:289
  55.7 47.7 %all-gather.12.cloned.1.call-done = bf16[2048,512]{1,0:T(8,128)(2,1)} async-done(((bf16[512,512]{1,0:T(8,128)(2,1)}), bf16[2048,512]{1,0:T(8,128)(2,1)}) %all-gather.12.cloned.1.call-update) | async-done | bytes 2097168 | tf_op jit(solution)/shard_map/all_gather | solution.py:291
  103.4 46.3 %all-gather.14.cloned.1.call-done = bf16[2048,512]{1,0:T(8,128)(2,1)} async-done(((bf16[512,512]{1,0:T(8,128)(2,1)}), bf16[2048,512]{1,0:T(8,128)(2,1)}) %all-gather.14.cloned.1.call-update) | async-done | bytes 2097168 | tf_op jit(solution)/shard_map/all_gather | solution.py:292
  149.7 80.9 %all-gather.10.cloned.1.call-done = bf16[16,256,512]{2,1,0:T(8,128)(2,1)} async-done(((bf16[4,256,512]{2,1,0:T(8,128)(2,1)}), bf16[16,256,512]{2,1,0:T(8,128)(2,1)}) %all-gather.10.cloned.1.call-update) | async-done | bytes 4194320 | tf_op jit(solution)/shard_map/all_gather | solution.py:288
  230.6 69.1 %forward.1 = (f32[4,256,512]{2,1,0:T(8,128)}, f32[4,256,512]{2,1,0:T(8,128)}, f32[4,256,512]{2,1,0:T(8,128)}, bf16[4,256,512]{2,1,0:T(8,128)(2,1)}, bf16[4,1024,...) custom-call(f32[1024,4]{1,0:T(8,128)} %copy.37.seg_ref, ...), custom_call_target="tpu_custom_call" | custom-call | tf_op jit(solution)/shard_map/forward/pallas_call | solution.py:349
  300.0 52.1 %backward.1 = (f32[4,256,512]{2,1,0:T(8,128)}, bf16[4,4,256,512]{3,2,1,0:T(8,128)(2,1)}, bf16[3,512,512]{2,1,0:T(8,128)(2,1)}) custom-call(f32[1024,4]{1,0:T(8,128)} %copy.37.seg_ref, f32[4,256]{1,0:T(4,128)} %dynamic-slice_bitcast_fusion.seg_own_ref, bf16[4,4,256,512]{3,2,1,0:T(8,128)(2,1)} %bitcast.47, bf16[4,256,512]{2,1,0:T(8,128)(2,1)} %bitcast.50, ...), custom_call_target="tpu_custom_call" | custom-call | tf_op jit(solution)/shard_map/backward/pallas_call | solution.py:376
  352.3 0.7 reduce-scatter.27.cloned.1.call-update
  353.0 0.7 reduce-scatter.23.cloned.1.call-update
  353.8 0.9 copy.46
  354.7 1.6 copy.44
  356.4 32.8 %reduce-scatter.19.cloned.1.call-done = bf16[3,64,512]{2,1,0:T(8,128)(2,1)} async-done(((bf16[3,512,512]{2,1,0:T(8,128)(2,1)}), bf16[3,64,512]{2,1,0:T(8,128)(2,1)}) %reduce-scatter.19.cloned.1.call-update) | async-done | bytes 196624 | tf_op jit(solution)/shard_map/reduce_scatter | solution.py:382
  389.2 1.2 copy.42
  390.5 1.0 reshape.34
  391.6 42.5 %reduce-scatter.27.cloned.1.call-done = bf16[4,64,512]{2,1,0:T(8,128)(2,1)} async-done(((bf16[4,512,512]{2,1,0:T(8,128)(2,1)}), bf16[4,64,512]{2,1,0:T(8,128)(2,1)}) %reduce-scatter.27.cloned.1.call-update) | async-done | bytes 262160 | tf_op jit(solution)/shard_map/reduce_scatter | solution.py:382
  434.2 44.5 %reduce-scatter.23.cloned.1.call-done = bf16[4,64,512]{2,1,0:T(8,128)(2,1)} async-done(((bf16[4,512,512]{2,1,0:T(8,128)(2,1)}), bf16[4,64,512]{2,1,0:T(8,128)(2,1)}) %reduce-scatter.23.cloned.1.call-update) | async-done | bytes 262160 | tf_op jit(solution)/shard_map/reduce_scatter | solution.py:382
  478.7 0.5 reduce-scatter.17.cloned.1.call-update
  479.2 1.1 copy-done.2
  480.3 2.7 copy.39
  483.0 2.7 copy.40
  485.6 129.2 %reduce-scatter.35.cloned.1.call-done = f32[16,4]{1,0:T(8,128)} async-done(((f32[512,4]{1,0:T(8,128)}), f32[16,4]{1,0:T(8,128)}) %reduce-scatter.35.cloned.1.call-update) | async-done | bytes 272
  614.8 0.9 fusion.1
  615.7 0.6 copy.51
  616.3 0.6 copy.50
  616.9 0.6 copy.49
  617.5 0.6 copy.48
  618.1 15.0 %reduce-scatter.33.cloned.1.call-done = bf16[128,64]{1,0:T(8,128)(2,1)} async-done(((bf16[512,64]{1,0:T(8,128)(2,1)}), bf16[128,64]{1,0:T(8,128)(2,1)}) %reduce-scatter.33.cloned.1.call-update) | async-done | bytes 16400
  633.0 0.8 copy.45
  633.9 0.6 convert_bitcast_fusion.1
  634.5 18.7 %reduce-scatter.31.cloned.1.call-done = bf16[128,192]{1,0:T(8,128)(2,1)} async-done(((bf16[512,192]{1,0:T(8,128)(2,1)}), bf16[128,192]{1,0:T(8,128)(2,1)}) %reduce-scatter.31.cloned.1.call-update) | async-done | bytes 49168
  653.2 0.9 reshape.35
  654.3 0.7 convert_element_type.26
  654.9 18.3 %reduce-scatter.29.cloned.1.call-done = bf16[1,64,512]{2,1,0:T(8,128)(2,1)} async-done(((bf16[4,64,512]{2,1,0:T(8,128)(2,1)}), bf16[1,64,512]{2,1,0:T(8,128)(2,1)}) %reduce-scatter.29.cloned.1.call-update) | async-done | bytes 65552 | tf_op jit(solution)/shard_map/reduce_scatter | solution.py:388
  673.2 1.5 convert_bitcast_fusion
  674.7 18.8 %reduce-scatter.25.cloned.1.call-done = bf16[1,64,512]{2,1,0:T(8,128)(2,1)} async-done(((bf16[4,64,512]{2,1,0:T(8,128)(2,1)}), bf16[1,64,512]{2,1,0:T(8,128)(2,1)}) %reduce-scatter.25.cloned.1.call-update) | async-done | bytes 65552 | tf_op jit(solution)/shard_map/reduce_scatter | solution.py:387
  693.5 1.5 bitcast_convert_fusion
  695.1 75.6 %reduce-scatter.17.cloned.1.call-done = bf16[1,4,256,512]{3,2,1,0:T(8,128)(2,1)} async-done(((bf16[4,4,256,512]{3,2,1,0:T(8,128)(2,1)}), bf16[1,4,256,512]{3,2,1,0:T(8,128)(2,1)}) %reduce-scatter.17.cloned.1.call-update) | async-done | bytes 1048592 | tf_op jit(solution)/shard_map/reduce_scatter | solution.py:379
  770.7 1.5 fusion
  772.2 2.7 copy.41
  (52 shorter events, 1.1 us)
Async XLA Ops:
  7.2 2.3 copy-start.3
  7.2 48.5 %all-gather.8.cloned.1.call-start = ((), (), s32[]{:S(2)}) async-start(), calls=%async_computation.10 | async-start | bytes 1966080 | tf_op jit(solution)/shard_map/all_gather | solution.py:289
  7.9 2.9 copy-start.8
  7.9 95.5 %all-gather.12.cloned.1.call-start = ((), (), s32[]{:S(2)}) async-start(), calls=%async_computation.19 | async-start | bytes 2621440 | tf_op jit(solution)/shard_map/all_gather | solution.py:291
  8.7 3.2 copy-start.4
  8.7 141.0 %all-gather.14.cloned.1.call-start = ((), (), s32[]{:S(2)}) async-start(), calls=%async_computation.20 | async-start | bytes 2621440 | tf_op jit(solution)/shard_map/all_gather | solution.py:292
  9.4 221.2 %all-gather.10.cloned.1.call-start = ((), (), s32[]{:S(2)}) async-start(), calls=%async_computation.18 | async-start | bytes 5242880 | tf_op jit(solution)/shard_map/all_gather | solution.py:288
  10.7 3.0 copy-start.10
  10.7 3.0 copy-start.11
  10.7 3.0 copy-start.12
  10.7 3.0 copy-start.13
  10.7 3.7 copy-start.7
  10.7 28.1 %copy-start.5 = (bf16[256,4,512]{2,1,0:T(4,128)(2,1)S(1)}, bf16[256,4,512]{2,1,0:T(4,128)(2,1)}, u32[]{:S(2)}) copy-start(bf16[256,4,512]{2,1,0:T(4,128)(2,1)} %param.16) | copy-start | bytes 3145732
  10.7 28.1 %copy-start.6 = (bf16[256,4,512]{2,1,0:T(4,128)(2,1)S(1)}, bf16[256,4,512]{2,1,0:T(4,128)(2,1)}, u32[]{:S(2)}) copy-start(bf16[256,4,512]{2,1,0:T(4,128)(2,1)} %param.15) | copy-start | bytes 3145732
  10.7 344.0 %reduce-scatter.21.cloned.1.call-start = ((), (), s32[]{:S(2)}) async-start(), calls=%async_computation.13 | async-start | bytes 589824 | tf_op jit(solution)/shard_map/reduce_scatter | solution.py:382
  299.8 89.4 %reduce-scatter.19.cloned.1.call-start = ((), (), s32[]{:S(2)}) async-start(), calls=%async_computation.12 | async-start | bytes 1769472 | tf_op jit(solution)/shard_map/reduce_scatter | solution.py:382
  352.2 81.9 %reduce-scatter.27.cloned.1.call-start = ((), (), s32[]{:S(2)}) async-start(), calls=%async_computation.16 | async-start | bytes 2359296 | tf_op jit(solution)/shard_map/reduce_scatter | solution.py:382
  352.2 1.5 copy-start.9
  352.9 125.7 %reduce-scatter.23.cloned.1.call-start = ((), (), s32[]{:S(2)}) async-start(), calls=%async_computation.14 | async-start | bytes 2359296 | tf_op jit(solution)/shard_map/reduce_scatter | solution.py:382
  353.7 261.1 %reduce-scatter.35.cloned.1.call-start = ((), (), s32[]{:S(2)}) async-start(), calls=%async_computation.23 | async-start | bytes 270336
  354.7 278.4 %reduce-scatter.33.cloned.1.call-start = ((), (), s32[]{:S(2)}) async-start(), calls=%async_computation.22 | async-start | bytes 163840
  356.4 296.9 %reduce-scatter.31.cloned.1.call-start = ((), (), s32[]{:S(2)}) async-start(), calls=%async_computation.21 | async-start | bytes 327680
  391.5 281.7 %reduce-scatter.29.cloned.1.call-start = ((), (), s32[]{:S(2)}) async-start(), calls=%async_computation.17 | async-start | bytes 327680 | tf_op jit(solution)/shard_map/reduce_scatter | solution.py:388
  434.1 259.4 %reduce-scatter.25.cloned.1.call-start = ((), (), s32[]{:S(2)}) async-start(), calls=%async_computation.15 | async-start | bytes 327680 | tf_op jit(solution)/shard_map/reduce_scatter | solution.py:387
  478.6 292.0 %reduce-scatter.17.cloned.1.call-start = ((), (), s32[]{:S(2)}) async-start(), calls=%async_computation.11 | async-start | bytes 5242880 | tf_op jit(solution)/shard_map/reduce_scatter | solution.py:379
  478.7 1.6 copy-start.2
  480.3 2.7 copy-start.1
  483.0 287.7 %copy-start = (f32[4,256,512]{2,1,0:T(8,128)S(1)}, f32[4,256,512]{2,1,0:T(8,128)}, u32[]{:S(2)}) copy-start(f32[4,256,512]{2,1,0:T(8,128)} %get-tuple-element.36) | copy-start | bytes 6291460
Sparse Core Ops, SparseCore 0:
  9.6 46.0 all-gather.7
  57.3 46.1 all-gather.11
  105.0 44.6 all-gather.13
  151.1 79.4 all-gather.9
  299.9 32.6 reduce-scatter.20
  352.3 36.8 reduce-scatter.18
  392.9 41.1 reduce-scatter.26
  437.4 41.2 reduce-scatter.22
  480.9 133.8 reduce-scatter.34
  617.5 15.5 reduce-scatter.32
  635.4 17.7 reduce-scatter.30
  655.4 17.8 reduce-scatter.28
  675.6 17.9 reduce-scatter.24
  695.7 74.9 reduce-scatter.16

commit v2 on v1

v2 whole, which is shorter than its diff:
```python
import functools
import itertools

import jax
import jax.numpy as jnp
from jax import lax
from jax.experimental import pallas as pl
from jax.experimental.pallas import tpu as pltpu
from jax.sharding import PartitionSpec as P

E = 64
EPSILON = 1e-05
NEGATIVE = -1e30
GELU_A = 0.7978845608028654
GELU_B = 0.044715
F32 = jnp.float32
BF16 = jnp.bfloat16
VMEM_BYTES = 63 * 1024 * 1024
LINKS = 256


def dot_nn(a, b):
    return lax.dot_general(a, b, (((1,), (0,)), ((), ())), preferred_element_type=F32)


def dot_nt(a, b):
    return lax.dot_general(a, b, (((1,), (1,)), ((), ())), preferred_element_type=F32)


def dot_tn(a, b):
    return lax.dot_general(a, b, (((0,), (0,)), ((), ())), preferred_element_type=F32)


def row_mean(a):
    return jnp.mean(a, axis=-1, keepdims=True)


def norm_forward(total):
    centre = total - row_mean(total)
    factor = lax.rsqrt(row_mean(centre * centre) + EPSILON)
    return centre * factor, factor


def norm_backward(upstream, normed, factor, gain):
    scaled = upstream * gain
    inner = scaled - row_mean(scaled) - normed * row_mean(scaled * normed)
    return factor * inner


def half_rows(block, half):
    zeros = jnp.zeros((E, block.shape[1]), block.dtype)
    if half == 0:
        return jnp.concatenate([block[:E], zeros], axis=0)
    return jnp.concatenate([zeros, block[E:]], axis=0)


MESH = pl.DeviceIdType.MESH


def bit_of(index, bit):
    return (index // (1 << bit)) % 2


def flip(index, mask):
    for bit in range(mask.bit_length()):
        if (mask >> bit) % 2:
            index = index + (1 - 2 * bit_of(index, bit)) * (1 << bit)
    return index


def log2(count):
    return count.bit_length() - 1


class Links:
    def __init__(self, send_sem, recv_sem):
        self.send_sem, self.recv_sem, self.used = send_sem, recv_sem, 0

    def take(self, count):
        first = self.used
        self.used += count
        assert self.used <= self.send_sem.shape[0]
        return first

    def copy(self, src, dst, slot, axis, partner):
        return pltpu.make_async_remote_copy(
            src_ref=src,
            dst_ref=dst,
            send_sem=self.send_sem.at[slot],
            recv_sem=self.recv_sem.at[slot],
            device_id={axis: partner},
            device_id_type=MESH,
        )


def start(copies):
    for copy in copies:
        copy.start()


def finish(copies):
    for copy in copies:
        copy.wait_recv()
        copy.wait_send()


def greet(dp_bits, tensors):
    dp, me = lax.axis_index("dp"), lax.axis_index("tensor")
    barrier = pltpu.get_barrier_semaphore()
    for bit in range(dp_bits):
        pl.semaphore_signal(barrier, inc=1, device_id={"dp": flip(dp, 1 << bit)}, device_id_type=MESH)
    for step in range(1, tensors):
        pl.semaphore_signal(
            barrier, inc=1, device_id={"tensor": (me + step) % tensors}, device_id_type=MESH
        )
    pl.semaphore_wait(barrier, dp_bits + tensors - 1)


class WeightGather:
    def __init__(self, links, src, dst, lead, cut_bits, dp_bits, first):
        tensors = dst.shape[0]
        dp, me = lax.axis_index("dp"), lax.axis_index("tensor")
        bits = list(range(dp_bits - 1, dp_bits - 1 - cut_bits, -1))
        self.src, self.dst, self.own = src, dst, me
        inner = [()] if lead == 0 else [(i,) for i in range(src.shape[0])]
        self.across = []
        for step in range(1, tensors):
            piece = (slice(None),) * lead + tuple(bit_of(dp, bit) for bit in bits)
            self.across.append(
                links.copy(
                    src.at[piece],
                    dst.at[(me,) + piece],
                    links.take(1),
                    "tensor",
                    (me + step) % tensors,
                )
            )
        low = [bit for bit in bits if bit == 0]
        high = [bit for bit in bits if bit != 0]
        orders = (high[::-1] + low, high + low)
        self.phases = [[] for _ in bits]
        count = first
        for step in range(1, tensors):
            source = (me + tensors - step) % tensors
            for i in inner:
                order = orders[count % 2]
                count += 1
                for phase, bit in enumerate(order):
                    done = order[:phase]
                    region = (source,) + i + tuple(
                        slice(None) if other in done else bit_of(dp, other) for other in bits
                    )
                    self.phases[phase].append(
                        links.copy(
                            dst.at[region],
                            dst.at[region],
                            links.take(1),
                            "dp",
                            flip(dp, 1 << bit),
                        )
                    )

    def own_copy(self, sem):
        return pltpu.make_async_copy(self.src, self.dst.at[self.own], sem)


class GradScatter:
    def __init__(self, links, grad, lands, across):
        self.links, self.grad, self.lands, self.across = links, grad, lands, across
        self.tensors = grad.shape[0]
        self.dp, self.me = lax.axis_index("dp"), lax.axis_index("tensor")
        dp_bits = len(lands)
        high = list(range(dp_bits - 1, 0, -1))
        middle = self.tensors // 2
        first = links.take(1)
        copies = [
            [
                links.copy(
                    grad.at[(slice(None),) * dp_bits + (1 - bit_of(self.dp, 0),)],
                    lands[0],
                    first,
                    "dp",
                    flip(self.dp, 1),
                )
            ]
        ]
        sums = [[(0, self.tensors, grad, dp_bits - 1, bit_of(self.dp, 0), lands[0])]]
        for step in range(1, dp_bits):
            copies.append([])
            sums.append([])
        for begin, order in ((0, high[::-1]), (middle, high)):
            left = list(high)
            for step, bit in enumerate(order, 1):
                place = left.index(bit)
                left.remove(bit)
                part = pl.ds(begin, middle)
                index = (part,) + (slice(None),) * place + (1 - bit_of(self.dp, bit),)
                copies[step].append(
                    links.copy(
                        lands[step - 1].at[index],
                        lands[step].at[part],
                        links.take(1),
                        "dp",
                        flip(self.dp, 1 << bit),
                    )
                )
                sums[step].append(
                    (begin, middle, lands[step - 1], place, bit_of(self.dp, bit), lands[step])
                )
        last = []
        for step in range(1, self.tensors):
            other = (self.me + step) % self.tensors
            last.append(
                links.copy(
                    lands[-1].at[other], across.at[step - 1], links.take(1), "tensor", other
                )
            )
        copies.append(last)
        self.copies, self.sums = copies, sums

    def begin(self):
        start(self.copies[0])

    def advance(self, step):
        finish(self.copies[step])
        for first, count, source, place, own, land in self.sums[step]:

            @pl.loop(first, first + count)
            def _(t):
                for spot in itertools.product((0, 1), repeat=len(land.shape) - 3):
                    whole = (t,) + spot[:place] + (own,) + spot[place:]
                    here = (t,) + spot
                    land[here] = (land[here].astype(F32) + source[whole].astype(F32)).astype(BF16)

        start(self.copies[step + 1])

    def result(self):
        finish(self.copies[-1])
        total = self.lands[-1][self.me].astype(F32)
        for step in range(self.tensors - 1):
            total = total + self.across[step].astype(F32)
        return total


class NormSum:
    def __init__(self, links, total, land, dp_bits, tensors):
        dp, me = lax.axis_index("dp"), lax.axis_index("tensor")
        self.total, self.land = total, land
        self.copies = [
            [links.copy(total, land.at[bit], links.take(1), "dp", flip(dp, 1 << bit))]
            for bit in range(dp_bits)
        ]
        self.copies.append(
            [
                links.copy(
                    total,
                    land.at[dp_bits + step - 1],
                    links.take(1),
                    "tensor",
                    (me + step) % tensors,
                )
                for step in range(1, tensors)
            ]
        )

    def begin(self):
        start(self.copies[0])

    def advance(self, step):
        finish(self.copies[step])
        self.total[...] += self.land[step]
        start(self.copies[step + 1])

    def result(self):
        finish(self.copies[-1])
        total = self.total[...]
        for step in range(len(self.copies) - 1, self.land.shape[0]):
            total = total + self.land[step]
        return total


def layer_kernel(
    dp_bits,
    columns,
    seg_ref,
    x_ref,
    dual_in_ref,
    cot_post_ref,
    cot_dual_ref,
    w_qkv_ref,
    w_out_ref,
    w_up_ref,
    w_down_ref,
    norms_ref,
    post_ref,
    dual_ref,
    grad_post_ref,
    r_qkv_ref,
    r_ffn_ref,
    r_norm_ref,
    x_col_ref,
    all_qkv_ref,
    all_out_ref,
    all_up_ref,
    all_down_ref,
    mixed_ref,
    do_ref,
    input_land_ref,
    g_ffn_ref,
    g_qkv_ref,
    ffn_lands,
    ffn_across_ref,
    qkv_lands,
    qkv_across_ref,
    norm_ref,
    norm_land_ref,
    q_ref,
    k_ref,
    v_ref,
    qt_ref,
    kt_ref,
    xt_ref,
    ot_ref,
    lse_ref,
    base_ref,
    stage_ref,
    bias_ref,
    send_sem,
    recv_sem,
    local_sem,
):
    tensors, rows, width = x_col_ref.shape
    owners = tensors // columns
    lanes = mixed_ref.shape[-1]
    heads = lanes // E
    pairs = heads // 2
    share = all_up_ref.shape[-1]
    shard = width // tensors
    last = tensors - 1
    length = tensors * rows
    tokens = columns * rows
    me = lax.axis_index("tensor")
    me_low = me % owners
    links = Links(send_sem, recv_sem)

    def slot_copies(sources, land):
        first = links.take(last)

        def one(slot, partner):
            source = sources.at[slot, :, pl.ds(0, land.shape[-1])]
            return links.copy(source, land.at[slot], first + slot, "tensor", partner)

        return one

    def partner_of(slot):
        mask = last - slot
        index = me
        for bit in range(log2(tensors)):
            index = index + bit_of(mask, bit) * (1 - 2 * bit_of(me, bit)) * (1 << bit)
        return index

    def gather(src, dst, lead, first):
        return WeightGather(links, src, dst, lead, len(src.shape) - lead - 2, dp_bits, first)

    qkv = gather(w_qkv_ref, all_qkv_ref, 1, 0)
    others = [
        gather(w_out_ref, all_out_ref, 0, 0),
        gather(w_up_ref, all_up_ref, 0, 0),
        gather(w_down_ref, all_down_ref, 0, 1),
    ]
    others_across = [copy for one in others for copy in one.across]
    others_phases = [
        [copy for one in others if len(one.phases) > phase for copy in one.phases[phase]]
        for phase in range(dp_bits)
    ]
    x_first = links.take(last)

    def x_copy(slot):
        partner = partner_of(slot)
        return links.copy(
            x_ref.at[partner // owners], x_col_ref.at[slot], x_first + slot, "tensor", partner
        )

    mixed_copy = slot_copies(stage_ref, mixed_ref)
    do_copy = slot_copies(stage_ref, do_ref)
    input_copy = slot_copies(stage_ref, input_land_ref)
    ffn_scatter = GradScatter(links, g_ffn_ref, ffn_lands, ffn_across_ref)
    qkv_scatter = GradScatter(links, g_qkv_ref, qkv_lands, qkv_across_ref)
    norm_sum = NormSum(links, norm_ref, norm_land_ref, dp_bits, tensors)

    local = [pltpu.make_async_copy(x_ref.at[me // owners], x_col_ref.at[last], local_sem.at[0])] + [
        one.own_copy(local_sem.at[1 + i]) for i, one in enumerate([qkv] + others)
    ]
    greet(dp_bits, tensors)
    start(qkv.across)
    start([x_copy(slot) for slot in range(last)])
    start(local)
    norm_ref[...] = jnp.zeros_like(norm_ref)
    if owners > 1:
        g_qkv_ref[...] = jnp.zeros_like(g_qkv_ref)
    finish(qkv.across)
    for copies in qkv.phases:
        start(copies)
        finish(copies)
    for copy in local:
        copy.wait()
    start(others_across)

    own_shards = pl.ds(me_low * (tensors // owners), tensors // owners)

    def w_t(i):
        return all_qkv_ref[own_shards, i].reshape(lanes, width)

    @pl.loop(0, tensors)
    def _(turn):
        slot = last - turn

        @pl.when(slot < last)
        def _():
            x_copy(slot).wait_recv()

        block = x_col_ref[slot]
        at = pl.ds(pl.multiple_of(slot * rows, rows), rows)
        q_ref[at, :] = dot_nt(block, w_t(0)).astype(BF16) * jnp.bfloat16(0.125)
        k_ref[at, :] = dot_nt(block, w_t(1)).astype(BF16)
        v_ref[at, :] = dot_nt(block, w_t(2)).astype(BF16)
        qt_ref[:, at] = dot_nt(w_t(0), block).astype(BF16) * jnp.bfloat16(0.125)
        kt_ref[:, at] = dot_nt(w_t(1), block).astype(BF16)
        xt_ref[:, at] = block.T

    seg_columns = seg_ref[...].T

    def bias_of(q_slot, k_slot):
        lane = lax.broadcasted_iota(jnp.int32, seg_columns.shape, 1)
        keys = jnp.sum(jnp.where(lane == k_slot, seg_columns, 0.0), axis=1, keepdims=True)
        return jnp.where(keys == seg_ref[pl.ds(q_slot, 1), :], 0.0, NEGATIVE)

    def forward_phase(
        vt_ref,
        hidden_ref,
        slope_ref,
        grad_inner_ref,
        up_two_ref,
        middle_ref,
        up_one_ref,
        home_ref,
        out_stage_ref,
    ):
        @pl.loop(0, tensors)
        def _(slot):
            at = pl.ds(pl.multiple_of(slot * rows, rows), rows)
            vt_ref[:, at] = dot_nt(w_t(2), x_col_ref[slot]).astype(BF16)

        @pl.loop(0, tensors)
        def _(slot):
            at_rows = pl.ds(pl.multiple_of(slot * rows, rows), rows)
            for k_slot in range(tensors):
                bias_ref[k_slot * rows : (k_slot + 1) * rows, :] = bias_of(slot, k_slot)

            @pl.loop(0, pairs)
            def _(j):
                @pl.when(slot == 0)
                def _():
                    for phase in range(dp_bits):

                        @pl.when(j == min(phase, pairs - 1))
                        def _():
                            finish(others_phases[phase - 1] if phase else others_across)
                            start(others_phases[phase])

                at = pl.ds(pl.multiple_of(j * 2 * E, 2 * E), 2 * E)
                keys = k_ref[:, at]
                queries = qt_ref[at, at_rows]
                for half in range(2):
                    scores = dot_nn(keys, half_rows(queries, half)) + bias_ref[...]
                    top = jnp.max(scores, axis=0, keepdims=True)
                    raised = jnp.exp(scores - top)
                    denom = jnp.sum(raised, axis=0, keepdims=True)
                    at_head = pl.ds(pl.multiple_of((2 * j + half) * E, E), E)
                    result = dot_nn(vt_ref[at_head, :], raised.astype(BF16))
                    ot_ref[slot, at_head, :] = result * (1.0 / denom)
                    lse_ref[slot, pl.ds(2 * j + half, 1), :] = top + jnp.log(denom)

            block = ot_ref[slot].T.astype(BF16)

            @pl.when(slot < last)
            def _():
                stage_ref[slot, :, :lanes] = block
                mixed_copy(slot, partner_of(slot)).start()

            @pl.when(slot == last)
            def _():
                mixed_ref[last] = block

        finish(others_phases[-1])
        gain_one, bias_one = norms_ref[0:1, :], norms_ref[1:2, :]
        gain_two, bias_two = norms_ref[2:3, :], norms_ref[3:4, :]

        @pl.loop(0, columns)
        def _(i):
            column = partner_of(owners * i) // owners
            loads = [
                pltpu.make_async_copy(ref.at[column], home_ref.at[n], local_sem.at[n])
                for n, ref in enumerate((x_ref, dual_in_ref, cot_post_ref, cot_dual_ref))
            ]
            start(loads)
            for r in range(owners):

                @pl.when(owners * i + r < last)
                def _():
                    mixed_copy(owners * i + r, partner_of(owners * i + r)).wait()

            def slot_of(h):
                return last - owners * (columns - 1 - i) - flip(me_low, h)

            mixed = jnp.concatenate([mixed_ref[slot_of(h)] for h in range(owners)], axis=1)
            at = pl.ds(pl.multiple_of(i * rows, rows), rows)
            branch_one = dot_nn(mixed, all_out_ref[...].reshape(width, width))
            for copy in loads:
                copy.wait()
            normed_one, factor_one = norm_forward(home_ref[0].astype(F32) + branch_one)
            middle = normed_one * gain_one + bias_one
            middle_low = middle.astype(BF16)
            middle_ref[:, at] = middle_low.T
            branch_two = jnp.zeros((rows, width), F32)
            for t in range(tensors):
                inner = dot_nn(middle_low, all_up_ref[t].reshape(width, share))
                square = inner * inner
                bend = jnp.tanh(GELU_A * (inner + GELU_B * (square * inner)))
                hidden = (0.5 * inner * (1.0 + bend)).astype(BF16)
                slope_ref[t] = 0.5 * (1.0 + bend) + (0.5 * GELU_A) * inner * (
                    1.0 - bend * bend
                ) * (1.0 + (3.0 * GELU_B) * square)
                hidden_ref[t, at, :] = hidden
                branch_two = branch_two + dot_nn(hidden, all_down_ref[t].reshape(share, width))
            normed_two, factor_two = norm_forward(middle + branch_two)
            stores = [
                pltpu.make_async_copy(out_stage_ref.at[n], ref.at[column], local_sem.at[4 + n])
                for n, ref in enumerate((post_ref, dual_ref))
            ]

            @pl.when(i > 0)
            def _():
                for copy in stores:
                    copy.wait()

            out_stage_ref[0] = normed_two * gain_two + bias_two
            out_stage_ref[1] = home_ref[1].astype(F32) + branch_one + branch_two
            start(stores)
            cot_dual = home_ref[3].astype(F32)
            upstream = home_ref[2].astype(F32)
            d_two = norm_backward(upstream, normed_two, factor_two, gain_two)
            norm_ref[2:3, :] += jnp.sum(upstream * normed_two, axis=0, keepdims=True)
            norm_ref[3:4, :] += jnp.sum(upstream, axis=0, keepdims=True)
            up_two = (d_two + cot_dual).astype(BF16)
            up_two_ref[:, at] = up_two.T
            grad_middle = d_two
            for t in range(tensors):
                grad_hidden = dot_nt(up_two, all_down_ref[t].reshape(share, width))
                grad_inner = (grad_hidden * slope_ref[t]).astype(BF16)
                grad_inner_ref[t, at, :] = grad_inner
                grad_middle = grad_middle + dot_nt(grad_inner, all_up_ref[t].reshape(width, share))
            d_one = norm_backward(grad_middle, normed_one, factor_one, gain_one)
            norm_ref[0:1, :] += jnp.sum(grad_middle * normed_one, axis=0, keepdims=True)
            norm_ref[1:2, :] += jnp.sum(grad_middle, axis=0, keepdims=True)
            base_ref[column] = d_one
            up_one = (d_one + cot_dual).astype(BF16)
            up_one_ref[:, at] = up_one.T
            grad_mixed = dot_nt(up_one, all_out_ref[...].reshape(width, width)).astype(BF16)
            for h in range(owners):
                slot = slot_of(h)
                piece = grad_mixed[:, h * lanes : (h + 1) * lanes]

                @pl.when(slot < last)
                def _():
                    stage_ref[slot, :, :lanes] = piece
                    do_copy(slot, partner_of(slot)).start()

                @pl.when(slot == last)
                def _():
                    do_ref[last] = piece

            @pl.when(i == columns - 1)
            def _():
                for copy in stores:
                    copy.wait()

        norm_sum.begin()
        cut = (2,) * dp_bits + (width >> dp_bits, share)

        @pl.loop(0, tensors)
        def _(t):
            g_down = dot_nn(up_two_ref[...], hidden_ref[t]).astype(BF16)
            g_up = dot_nn(middle_ref[...], grad_inner_ref[t]).astype(BF16)
            at_t = (t,) + (slice(None),) * (dp_bits + 1)
            g_ffn_ref[at_t + (slice(0, share),)] = g_down.reshape(cut)
            g_ffn_ref[at_t + (slice(share, 2 * share),)] = g_up.reshape(cut)

        def mixed_of(i):
            def slot_of(h):
                return last - owners * (columns - 1 - i) - flip(me_low, h)

            return jnp.concatenate([mixed_ref[slot_of(h)] for h in range(owners)], axis=1)

        all_mixed = jnp.concatenate([mixed_of(i) for i in range(columns)], axis=0)
        g_out = dot_nn(up_one_ref[...], all_mixed).astype(BF16)
        for t in range(tensors):
            g_ffn_ref[
                (t,) + (slice(None),) * (dp_bits + 1) + (slice(2 * share, 2 * share + shard),)
            ] = g_out[:, t * shard : (t + 1) * shard].reshape(cut[:-1] + (shard,))
        ffn_scatter.begin()

    pl.run_scoped(
        forward_phase,
        pltpu.VMEM((lanes, length), BF16),
        pltpu.VMEM((tensors, tokens, share), BF16),
        pltpu.VMEM((tensors, rows, share), F32),
        pltpu.VMEM((tensors, tokens, share), BF16),
        pltpu.VMEM((width, tokens), BF16),
        pltpu.VMEM((width, tokens), BF16),
        pltpu.VMEM((width, tokens), BF16),
        pltpu.VMEM((4, rows, width), BF16),
        pltpu.VMEM((2, rows, width), F32),
    )

    def backward_phase(dot_ref, delta_ref, dq_ref, dk_ref, dv_ref, grads_ref):
        dq_ref[...] = jnp.zeros_like(dq_ref)
        dk_ref[...] = jnp.zeros_like(dk_ref)
        dv_ref[...] = jnp.zeros_like(dv_ref)

        @pl.loop(0, tensors)
        def _(slot):
            @pl.when(slot < last)
            def _():
                do_copy(slot, partner_of(slot)).wait()

            at = pl.ds(pl.multiple_of(slot * rows, rows), rows)
            turned = do_ref[slot].T
            dot_ref[:, at] = turned
            product = turned.astype(F32) * ot_ref[slot]
            delta_ref[slot, :heads] = jnp.sum(product.reshape(heads, E, rows), axis=1)

        def pair_of(q_slot, k_slot):
            at_q = pl.ds(pl.multiple_of(q_slot * rows, rows), rows)
            at_k = pl.ds(pl.multiple_of(k_slot * rows, rows), rows)
            bias_ref[:rows, :] = bias_of(q_slot, k_slot)

            @pl.loop(0, pairs)
            def _(j):
                at = pl.ds(pl.multiple_of(j * 2 * E, 2 * E), 2 * E)
                keys, values = k_ref[at_k, at], v_ref[at_k, at]
                queries, ups = q_ref[at_q, at], do_ref[q_slot, :, at]
                sums = []
                for half in range(2):
                    row = pl.ds(2 * j + half, 1)
                    scores = dot_nn(keys, half_rows(qt_ref[at, at_q], half)) + bias_ref[:rows, :]
                    probs = jnp.exp(scores - lse_ref[q_slot, row, :])
                    pushed = dot_nn(values, half_rows(dot_ref[at, at_q], half))
                    delta = (probs * (pushed - delta_ref[q_slot, row, :])).astype(BF16)
                    at_head = pl.ds(pl.multiple_of((2 * j + half) * E, E), E)
                    dq_ref[at_head, at_q] += dot_nn(kt_ref[at_head, at_k], delta)
                    sums.append((dot_nn(delta, queries), dot_nn(probs.astype(BF16), ups)))
                low_half = lax.broadcasted_iota(jnp.int32, sums[0][0].shape, 1) < E
                dk_ref[at_k, at] += jnp.where(low_half, sums[0][0], sums[1][0])
                dv_ref[at_k, at] += jnp.where(low_half, sums[0][1], sums[1][1])

        @pl.loop(0, tensors)
        def _(wave):
            for step in range(1, dp_bits):

                @pl.when(wave == step)
                def _():
                    ffn_scatter.advance(step)
                    norm_sum.advance(step)

            @pl.loop(wave, tensors)
            def _(k_slot):
                @pl.when((wave == 0) & (k_slot == 1))
                def _():
                    ffn_scatter.advance(0)
                    norm_sum.advance(0)

                pair_of(wave, k_slot)

            @pl.loop(wave + 1, tensors)
            def _(q_slot):
                pair_of(q_slot, wave)

            at = pl.ds(pl.multiple_of(wave * rows, rows), rows)
            grads = (
                (dq_ref[:, at] * 0.125).T.astype(BF16),
                dk_ref[at, :].astype(BF16),
                dv_ref[at, :].astype(BF16),
            )
            part = jnp.zeros((rows, width), F32)
            for i in range(3):
                grads_ref[i, at, :] = grads[i]
                part = part + dot_nn(grads[i], w_t(i))

            @pl.when(wave < last)
            def _():
                stage_ref[wave] = part.astype(BF16)
                input_copy(wave, partner_of(wave)).start()

            @pl.when(wave == last)
            def _():
                base_ref[me // owners] += part

        for i in range(3):
            g = dot_nn(xt_ref[...], grads_ref[i]).astype(BF16)
            for t in range(tensors // owners):
                index = (me_low * (tensors // owners) + t,) + (slice(None),) * (dp_bits + 1)
                g_qkv_ref[index + (slice(i * shard, (i + 1) * shard),)] = g[
                    :, t * shard : (t + 1) * shard
                ].reshape((2,) * dp_bits + (width >> dp_bits, shard))

    pl.run_scoped(
        backward_phase,
        pltpu.VMEM((lanes, length), BF16),
        pltpu.VMEM((tensors, max(heads, 8), rows), F32),
        pltpu.VMEM((lanes, length), F32),
        pltpu.VMEM((length, lanes), F32),
        pltpu.VMEM((length, lanes), F32),
        pltpu.VMEM((3, length, lanes), BF16),
    )

    qkv_scatter.begin()
    for slot in range(last):
        x_copy(slot).wait_send()

    @pl.loop(0, last)
    def _(slot):
        input_copy(slot, partner_of(slot)).wait()
        base_ref[partner_of(slot) // owners] += input_land_ref[slot].astype(F32)

    stored = pltpu.make_async_copy(base_ref, grad_post_ref, local_sem.at[0])
    stored.start()
    qkv_scatter.advance(0)
    r_ffn_ref[...] = ffn_scatter.result()
    r_norm_ref[...] = norm_sum.result()
    for step in range(1, dp_bits):
        qkv_scatter.advance(step)
    r_qkv_ref[...] = qkv_scatter.result()
    stored.wait()


def body(
    x_post,
    x_dual,
    cot_post,
    cot_dual,
    segment_ids,
    w_qkv,
    w_out,
    w_up,
    w_down,
    gain_one,
    bias_one,
    gain_two,
    bias_two,
):
    tensors, devices = lax.axis_size("tensor"), lax.axis_size("dp")
    dp_bits = log2(devices)
    rows, columns, width = x_post.shape
    length = tensors * rows
    owners = tensors // columns
    lanes = width // owners
    share, shard = w_up.shape[1], w_out.shape[0]
    piece = width // devices
    heads = lanes // E
    me = lax.axis_index("tensor")
    norms = jnp.stack([gain_one, bias_one, gain_two, bias_two])

    def cut(array, dim):
        bits = min(dp_bits, log2(array.shape[dim] // 16))
        shape = array.shape[:dim] + (2,) * bits + (array.shape[dim] >> bits,) + array.shape[dim + 1 :]
        return array.reshape(shape)

    shards = [cut(jnp.swapaxes(w_qkv, 1, 2), 1), cut(w_out, 0), cut(w_up, 0), cut(w_down, 0)]
    own = lax.dynamic_slice_in_dim(segment_ids.T, me // owners, 1, axis=0).reshape(tensors, rows)
    seg = jnp.stack(
        [
            lax.dynamic_index_in_dim(own, flip(me, tensors - 1 - slot), 0, keepdims=False)
            for slot in range(tensors)
        ]
    ).astype(F32)
    seg = jnp.pad(seg, ((0, -tensors % 8), (0, 0)))
    in_vmem = pl.BlockSpec(memory_space=pltpu.VMEM)
    in_place = pl.BlockSpec(memory_space=pl.ANY)
    shape = jax.ShapeDtypeStruct
    bits = (2,) * dp_bits
    ffn_lanes = 2 * share + shard

    def lands(lane_count):
        return [
            pltpu.VMEM((tensors,) + bits[: dp_bits - 1 - step] + (piece, lane_count), BF16)
            for step in range(dp_bits)
        ]

    layer = pl.pallas_call(
        functools.partial(layer_kernel, dp_bits, columns),
        out_shape=(
            shape((columns, rows, width), F32),
            shape((columns, rows, width), F32),
            shape((columns, rows, width), F32),
            shape((piece, 3 * shard), F32),
            shape((piece, ffn_lanes), F32),
            shape((8, width), F32),
        ),
        in_specs=[in_vmem] + [in_place] * 8 + [in_vmem],
        out_specs=(in_place,) * 3 + (in_vmem,) * 3,
        scratch_shapes=[pltpu.VMEM((tensors, rows, width), BF16)]
        + [pltpu.VMEM((tensors,) + one.shape, BF16) for one in shards]
        + [
            pltpu.VMEM((tensors, rows, lanes), BF16),
            pltpu.VMEM((tensors, rows, lanes), BF16),
            pltpu.VMEM((tensors - 1, rows, width), BF16),
            pltpu.VMEM((tensors,) + bits + (piece, ffn_lanes), BF16),
            pltpu.VMEM((tensors,) + bits + (piece, 3 * shard), BF16),
            lands(ffn_lanes),
            pltpu.VMEM((tensors - 1, piece, ffn_lanes), BF16),
            lands(3 * shard),
            pltpu.VMEM((tensors - 1, piece, 3 * shard), BF16),
            pltpu.VMEM((8, width), F32),
            pltpu.VMEM((dp_bits + tensors - 1, 8, width), F32),
            pltpu.VMEM((length, lanes), BF16),
            pltpu.VMEM((length, lanes), BF16),
            pltpu.VMEM((length, lanes), BF16),
            pltpu.VMEM((lanes, length), BF16),
            pltpu.VMEM((lanes, length), BF16),
            pltpu.VMEM((width, length), BF16),
            pltpu.VMEM((tensors, lanes, rows), F32),
            pltpu.VMEM((tensors, max(heads, 8), rows), F32),
            pltpu.VMEM((columns, rows, width), F32),
            pltpu.VMEM((tensors - 1, rows, width), BF16),
            pltpu.VMEM((length, rows), F32),
            pltpu.SemaphoreType.DMA((LINKS,)),
            pltpu.SemaphoreType.DMA((LINKS,)),
            pltpu.SemaphoreType.DMA((8,)),
        ],
        compiler_params=pltpu.CompilerParams(
            vmem_limit_bytes=VMEM_BYTES, collective_id=0, has_side_effects=True
        ),
        name="layer",
    )
    post_out, dual_out, grad_post, r_qkv, r_ffn, r_norm = layer(
        seg,
        jnp.swapaxes(x_post, 0, 1),
        jnp.swapaxes(x_dual, 0, 1),
        jnp.swapaxes(cot_post, 0, 1),
        jnp.swapaxes(cot_dual, 0, 1),
        *shards,
        norms,
    )
    count = width // (tensors * devices)
    own_norms = lax.dynamic_slice_in_dim(
        r_norm, (lax.axis_index("dp") * tensors + me) * count, count, axis=1
    )
    return (
        jnp.swapaxes(post_out, 0, 1),
        jnp.swapaxes(dual_out, 0, 1),
        jnp.swapaxes(grad_post, 0, 1),
        jnp.swapaxes(r_qkv.reshape(piece, 3, shard), 0, 1),
        r_ffn[:, 2 * share :].T,
        r_ffn[:, share : 2 * share],
        r_ffn[:, :share].T,
        own_norms[0],
        own_norms[1],
        own_norms[2],
        own_norms[3],
    )


def solution(mesh):
    placed = (
        P("tensor", "dp", None),
        P("tensor", "dp", None),
        P("tensor", "dp", None),
        P("tensor", "dp", None),
        P(None, "dp"),
        P(None, None, "tensor"),
        P("tensor", None),
        P(None, "tensor"),
        P("tensor", None),
        P(),
        P(),
        P(),
        P(),
    )
    return jax.shard_map(
        body,
        mesh=mesh,
        in_specs=placed,
        out_specs=(
            P("tensor", "dp", None),
            P("tensor", "dp", None),
            P("tensor", "dp", None),
            P(None, "dp", "tensor"),
            P("tensor", "dp"),
            P("dp", "tensor"),
            P("tensor", "dp"),
            P(("dp", "tensor")),
            P(("dp", "tensor")),
            P(("dp", "tensor")),
            P(("dp", "tensor")),
        ),
        check_vma=False,
    )
```

time: 782 us -> 226 us (0.29)
  waiting for transfers between devices: 590 us -> 0 us
  Pallas kernels: 121 us -> 202 us
  blocking collectives: 24.4 us -> 0 us
  between operations: 14.1 us -> 0.81 us
    reduce_scatter x7 -> x0, waiting for transfers between devices: 233 us -> none  [the longest x4 120 us: over_dp(): return lax.psum_scatter(array, 'dp', scatter_dimension=dim, tiled=True)]
    all_gather x4 -> x0, waiting for transfers between devices: 190 us -> none  [the longest x1 80.9 us: body(): x_all = lax.all_gather(x_own, 'tensor', axis=0)]
    unnamed x17 -> x0, waiting for transfers between devices: 167 us -> none
    pallas_call x2 -> x1, Pallas kernels: 121 us -> 202 us  [body(): layer(seg, jnp.swapaxes(x_post, 0, 1), jnp.swapaxes(x_dual, 0, 1), jnp.sw...]
    all_gather x1 -> x0, blocking collectives: 24.4 us -> none  [body(): all_out = lax.all_gather(w_out, 'tensor', axis=0, tiled=True)]
    unnamed x44 -> x18, local copies, waits for them, and re-layouts: 20.6 us -> 11 us
  transfers between devices with their start and end apart: 14 -> 0, of which waited for: 13 -> 0; matrix products, arithmetic and copies ran while one was open for 3% -> 0% of each run, Pallas kernels for 7% -> 0%
where the time goes in v2:
time: 226 us
  Pallas kernels  202 us (89%)
  local copies, waits for them, and re-layouts  21.4 us (9%)
    pallas_call x1, Pallas kernels, body(): layer(seg, jnp.swapaxes(x_post, 0, 1), jnp.swapaxes(x_dual, 0, 1), jnp.sw...  202 us
    unnamed x18, local copies, waits for them, and re-layouts  11 us

profile of v2, /device:TPU:0, one launch (start us, length us, event | category | flops | bytes accessed | tf_op | source)
XLA Modules:
  0.0 226.0 jit_solution(17372112011753121625)
XLA Ops:
  0.6 0.0 copy-start
  0.8 0.6 copy-done
  1.4 0.6 pad.4.seg_ref
  2.0 1.3 pad_maximum_fusion.norms_ref
  3.4 1.9 copy.37
  5.3 0.0 copy-start.3
  5.3 0.0 copy-start.4
  5.3 3.4 %copy_bitcast_fusion.2 = (bf16[4,256,512]{2,1,0:T(8,128)(2,1)}, bf16[4,256,512]{2,1,0:T(8,128)(2,1)}) fusion(bf16[256,4,512]{2,1,0:T(4,128)(2,1)} %param.14, bf16[256,4,512]{2,1,0:T(4,128)(2,1)} %param.13), kind=kLoop, calls=%fused_computation.2 | loop fusion | bytes 4194304 | tf_op jit(solution)/shard_map/transpose | solution.py:849
  8.7 0.0 copy-done.3
  8.7 0.0 copy-done.4
  8.7 1.8 copy_bitcast_fusion
  10.5 202.4 %layer.1 = (f32[4,256,512]{2,1,0:T(8,128)}, f32[4,256,512]{2,1,0:T(8,128)}, f32[4,256,512]{2,1,0:T(8,128)}, f32[64,384]{1,0:T(8,128)}, f32[64,1152]{1,0:T(8,128)}, /*index=5*/f32[8,512]{1,0:T(8,128)}) custom-call(f32[8,256]{1,0:T(8,128)} %pad.4.seg_ref, bf16[4,256,512]{2,1,0:T(8,128)(2,1)} %get-tuple-element.58.x_ref, ...), custom_call_target="tpu_custom_call" | custom-call | tf_op jit(solution)/shard_map/layer/pallas_call | solution.py:846
  212.9 0.0 copy-start.2
  213.0 4.4 %copy.38 = f32[256,4,512]{2,1,0:T(4,128)} copy(f32[256,4,512]{2,0,1:T(8,128)} %bitcast.35) | data formatting | bytes 4194304
  217.4 0.0 copy-done.2
  217.4 0.0 copy-start.5
  217.4 0.0 copy-start.6
  217.4 0.0 copy-start.1
  217.4 2.7 %copy.39 = f32[256,4,512]{2,1,0:T(4,128)} copy(f32[256,4,512]{2,0,1:T(8,128)S(1)} %bitcast.34) | data formatting | bytes 4194304
  220.0 0.7 constant_dynamic-slice_fusion
  220.8 0.5 slice_bitcast_fusion.2
  221.3 0.0 copy-done.5
  221.3 0.6 slice_bitcast_fusion.1
  221.9 0.7 slice_bitcast_fusion
  222.7 0.0 copy-done.6
  222.7 0.6 copy.41
  223.4 0.0 copy-done.1
  223.4 2.7 %copy.40 = f32[256,4,512]{2,1,0:T(4,128)} copy(f32[256,4,512]{2,0,1:T(8,128)S(1)} %bitcast.33) | data formatting | bytes 4194304
  (5 shorter events, 0.1 us)
Async XLA Ops:
  0.6 0.7 copy-start
  5.3 3.4 %copy-start.3 = (bf16[256,4,512]{2,1,0:T(4,128)(2,1)S(1)}, bf16[256,4,512]{2,1,0:T(4,128)(2,1)}, u32[]{:S(2)}) copy-start(bf16[256,4,512]{2,1,0:T(4,128)(2,1)} %param.16) | copy-start | bytes 3145732
  5.3 3.4 %copy-start.4 = (bf16[256,4,512]{2,1,0:T(4,128)(2,1)S(1)}, bf16[256,4,512]{2,1,0:T(4,128)(2,1)}, u32[]{:S(2)}) copy-start(bf16[256,4,512]{2,1,0:T(4,128)(2,1)} %param.15) | copy-start | bytes 3145732
  212.9 4.4 %copy-start.2 = (f32[4,256,512]{2,1,0:T(8,128)S(1)}, f32[4,256,512]{2,1,0:T(8,128)}, u32[]{:S(2)}) copy-start(f32[4,256,512]{2,1,0:T(8,128)} %get-tuple-element.18) | copy-start | bytes 6291460
  217.4 3.9 %copy-start.5 = (f32[64,1152]{1,0:T(8,128)S(1)}, f32[64,1152]{1,0:T(8,128)}, u32[]{:S(2)}) copy-start(f32[64,1152]{1,0:T(8,128)} %get-tuple-element.21) | copy-start | bytes 884740
  217.4 5.3 %copy-start.6 = (f32[64,384]{1,0:T(8,128)S(1)}, f32[64,384]{1,0:T(8,128)}, u32[]{:S(2)}) copy-start(f32[64,384]{1,0:T(8,128)} %get-tuple-element.20) | copy-start | bytes 294916
  217.4 6.0 %copy-start.1 = (f32[4,256,512]{2,1,0:T(8,128)S(1)}, f32[4,256,512]{2,1,0:T(8,128)}, u32[]{:S(2)}) copy-start(f32[4,256,512]{2,1,0:T(8,128)} %get-tuple-element.19) | copy-start | bytes 6291460

commit v3 on v2

v3 whole, which is shorter than its diff:
```python
import functools
import itertools

import jax
import jax.numpy as jnp
from jax import lax
from jax.experimental import pallas as pl
from jax.experimental.pallas import tpu as pltpu
from jax.sharding import PartitionSpec as P

E = 64
EPSILON = 1e-05
NEGATIVE = -1e30
DOCUMENTS = 4
DOWN_DUES = (0.06, 0.35, 0.75)
UP_DUES = (0.10, 0.5, 0.9)
GATHER_DUE, GATHER_LEVEL, GATHER_STEP = 6, 4, 3
PARTS = 3
GELU_A = 0.7978845608028654
GELU_B = 0.044715
F32 = jnp.float32
BF16 = jnp.bfloat16
VMEM_BYTES = 63 * 1024 * 1024
LINKS = 320


def dot_nn(a, b):
    return lax.dot_general(a, b, (((1,), (0,)), ((), ())), preferred_element_type=F32)


def dot_nt(a, b):
    return lax.dot_general(a, b, (((1,), (1,)), ((), ())), preferred_element_type=F32)


def dot_tn(a, b):
    return lax.dot_general(a, b, (((0,), (0,)), ((), ())), preferred_element_type=F32)


def row_mean(a):
    return jnp.mean(a, axis=-1, keepdims=True)


def norm_forward(total):
    centre = total - row_mean(total)
    factor = lax.rsqrt(row_mean(centre * centre) + EPSILON)
    return centre * factor, factor


def norm_backward(upstream, normed, factor, gain):
    scaled = upstream * gain
    inner = scaled - row_mean(scaled) - normed * row_mean(scaled * normed)
    return factor * inner


def with_marks(block, marks):
    return jnp.concatenate([block, marks], axis=0)


def with_row(marks, row):
    line = lax.broadcasted_iota(jnp.int32, (16, row.shape[1]), 0)
    top = marks[:16].astype(F32)
    rest = -row
    for part in range(PARTS):
        term = rest.astype(BF16).astype(F32)
        rest = rest - term
        top = jnp.where(line == DOCUMENTS + part, term, top)
    return jnp.concatenate([top.astype(BF16), marks[16:]], axis=0)


def half_rows(block, half):
    zeros = jnp.zeros((E, block.shape[1]), block.dtype)
    if half == 0:
        return jnp.concatenate([block[:E], zeros], axis=0)
    return jnp.concatenate([zeros, block[E:]], axis=0)


MESH = pl.DeviceIdType.MESH


def bit_of(index, bit):
    return (index // (1 << bit)) % 2


def flip(index, mask):
    for bit in range(mask.bit_length()):
        if (mask >> bit) % 2:
            index = index + (1 - 2 * bit_of(index, bit)) * (1 << bit)
    return index


def log2(count):
    return count.bit_length() - 1


class Links:
    def __init__(self, send_sem, recv_sem):
        self.send_sem, self.recv_sem, self.used = send_sem, recv_sem, 0

    def take(self, count):
        first = self.used
        self.used += count
        assert self.used <= self.send_sem.shape[0]
        return first

    def copy(self, src, dst, slot, axis, partner):
        return pltpu.make_async_remote_copy(
            src_ref=src,
            dst_ref=dst,
            send_sem=self.send_sem.at[slot],
            recv_sem=self.recv_sem.at[slot],
            device_id={axis: partner},
            device_id_type=MESH,
        )


def start(copies):
    for copy in copies:
        copy.start()


def finish(copies):
    for copy in copies:
        copy.wait_recv()
        copy.wait_send()


def greet(dp_bits, tensors):
    dp, me = lax.axis_index("dp"), lax.axis_index("tensor")
    barrier = pltpu.get_barrier_semaphore()
    for bit in range(dp_bits):
        pl.semaphore_signal(barrier, inc=1, device_id={"dp": flip(dp, 1 << bit)}, device_id_type=MESH)
    for step in range(1, tensors):
        pl.semaphore_signal(
            barrier, inc=1, device_id={"tensor": (me + step) % tensors}, device_id_type=MESH
        )


def greeted(dp_bits, tensors):
    pl.semaphore_wait(pltpu.get_barrier_semaphore(), dp_bits + tensors - 1)


class WeightGather:
    def __init__(self, links, src, dst, lead, cut_bits, dp_bits, first, direct):
        tensors = dst.shape[0]
        dp, me = lax.axis_index("dp"), lax.axis_index("tensor")
        bits = list(range(dp_bits - 1, dp_bits - 1 - cut_bits, -1))
        if src is None:
            src = dst.at[me]
        self.src, self.dst, self.own = src, dst, me
        inner = [()] if lead == 0 else [(i,) for i in range(dst.shape[1])]
        piece = (slice(None),) * lead + tuple(bit_of(dp, bit) for bit in bits)
        low = [bit for bit in bits if bit == 0]
        high = [bit for bit in bits if bit != 0]
        orders = (high[::-1] + low, high + low)
        count = first
        self.stages = {}
        for mask in range(1, tensors):
            near = mask if direct else mask & -mask
            block = flip(me, mask - near)
            stages = [[] for _ in range(1 + dp_bits)]
            stages[0].append(
                links.copy(
                    dst.at[(block,) + piece] if mask != near else src.at[piece],
                    dst.at[(block,) + piece],
                    links.take(1),
                    "tensor",
                    flip(me, near),
                )
            )
            source = flip(me, mask)
            for i in inner:
                order = orders[count % 2]
                count += 1
                for phase, bit in enumerate(order):
                    done = order[:phase]
                    region = (source,) + i + tuple(
                        slice(None) if other in done else bit_of(dp, other) for other in bits
                    )
                    stages[1 + phase].append(
                        links.copy(
                            dst.at[region],
                            dst.at[region],
                            links.take(1),
                            "dp",
                            flip(dp, 1 << bit),
                        )
                    )
            self.stages[mask] = stages

    def own_copy(self, sem):
        return pltpu.make_async_copy(self.src, self.dst.at[self.own], sem)


class Stages:
    def __init__(self, weights, masks):
        count = len(weights[0].stages[masks[0]])
        self.copies = [
            [copy for one in weights for mask in masks for copy in one.stages[mask][stage]]
            for stage in range(count)
        ]
        self.count = count

    def begin(self):
        start(self.copies[0])

    def advance(self, stage):
        finish(self.copies[stage])
        if stage + 1 < self.count:
            start(self.copies[stage + 1])


class GradScatter:
    def __init__(self, links, grad, lands, across, direct):
        self.links, self.grad, self.lands, self.across = links, grad, lands, across
        self.tensors = grad.shape[0]
        self.dp, self.me = lax.axis_index("dp"), lax.axis_index("tensor")
        dp_bits = len(lands)
        high = list(range(dp_bits - 1, 0, -1))
        middle = self.tensors // 2
        first = links.take(1)
        copies = [
            [
                links.copy(
                    grad.at[(slice(None),) * dp_bits + (1 - bit_of(self.dp, 0),)],
                    lands[0],
                    first,
                    "dp",
                    flip(self.dp, 1),
                )
            ]
        ]
        sums = [[(0, self.tensors, grad, dp_bits - 1, bit_of(self.dp, 0), lands[0])]]
        for step in range(1, dp_bits):
            copies.append([])
            sums.append([])
        for begin, order in ((0, high[::-1]), (middle, high)):
            left = list(high)
            for step, bit in enumerate(order, 1):
                place = left.index(bit)
                left.remove(bit)
                part = pl.ds(begin, middle)
                index = (part,) + (slice(None),) * place + (1 - bit_of(self.dp, bit),)
                copies[step].append(
                    links.copy(
                        lands[step - 1].at[index],
                        lands[step].at[part],
                        links.take(1),
                        "dp",
                        flip(self.dp, 1 << bit),
                    )
                )
                sums[step].append(
                    (begin, middle, lands[step - 1], place, bit_of(self.dp, bit), lands[step])
                )
        place = 0
        self.joins = []
        for bit in range(0 if direct else log2(self.tensors)):
            step, found, joins = 1 << bit, [], []
            for high in range(self.tensors >> (bit + 1)):
                mask = high * 2 * step
                found.append(
                    links.copy(
                        lands[-1].at[flip(self.me, mask + step)],
                        across.at[place],
                        links.take(1),
                        "tensor",
                        flip(self.me, step),
                    )
                )
                joins.append((mask, place))
                place += 1
            copies.append(found)
            self.joins.append(joins)
        if direct:
            copies.append(
                [
                    links.copy(
                        lands[-1].at[flip(self.me, step)],
                        across.at[step - 1],
                        links.take(1),
                        "tensor",
                        flip(self.me, step),
                    )
                    for step in range(1, self.tensors)
                ]
            )
            self.joins = [[(0, step) for step in range(self.tensors - 1)]]
        self.copies, self.sums = copies, sums + [[] for _ in self.joins[1:]]
        self.steps = len(copies) - 1

    def begin(self):
        start(self.copies[0])

    def advance(self, step):
        finish(self.copies[step])
        for first, count, source, place, own, land in self.sums[step]:

            @pl.loop(first, first + count)
            def _(t):
                for spot in itertools.product((0, 1), repeat=len(land.shape) - 3):
                    whole = (t,) + spot[:place] + (own,) + spot[place:]
                    here = (t,) + spot
                    land[here] = (land[here].astype(F32) + source[whole].astype(F32)).astype(BF16)

        if step >= len(self.lands):
            for mask, place in self.joins[step - len(self.lands)]:
                spot = flip(self.me, mask)
                total = self.lands[-1][spot].astype(F32) + self.across[place].astype(F32)
                self.lands[-1][spot] = total.astype(BF16)
        start(self.copies[step + 1])

    def result(self):
        finish(self.copies[-1])
        total = self.lands[-1][self.me].astype(F32)
        for _, place in self.joins[-1]:
            total = total + self.across[place].astype(F32)
        return total


class NormSum:
    def __init__(self, links, total, land, dp_bits, tensors):
        dp, me = lax.axis_index("dp"), lax.axis_index("tensor")
        self.total, self.land = total, land
        self.copies = [
            [links.copy(total, land.at[bit], links.take(1), "dp", flip(dp, 1 << bit))]
            for bit in range(dp_bits)
        ]
        self.copies.append(
            [
                links.copy(
                    total,
                    land.at[dp_bits + step - 1],
                    links.take(1),
                    "tensor",
                    (me + step) % tensors,
                )
                for step in range(1, tensors)
            ]
        )

    def begin(self):
        start(self.copies[0])

    def advance(self, step):
        if step + 1 < len(self.copies):
            finish(self.copies[step])
            self.total[...] += self.land[step]
            start(self.copies[step + 1])

    def result(self):
        finish(self.copies[-1])
        total = self.total[...]
        for step in range(len(self.copies) - 1, self.land.shape[0]):
            total = total + self.land[step]
        return total


def layer_kernel(
    dp_bits,
    columns,
    seg_ref,
    x_ref,
    dual_in_ref,
    cot_post_ref,
    cot_dual_ref,
    w_qkv_ref,
    w_out_ref,
    w_up_ref,
    w_down_ref,
    gain_one_ref,
    bias_one_ref,
    gain_two_ref,
    bias_two_ref,
    post_ref,
    dual_ref,
    grad_post_ref,
    r_qkv_ref,
    r_down_ref,
    r_up_ref,
    r_norm_ref,
    home_ref,
    x_col_ref,
    all_qkv_ref,
    all_out_ref,
    all_up_ref,
    all_down_ref,
    mixed_ref,
    do_ref,
    input_land_ref,
    g_down_ref,
    g_up_ref,
    g_qkv_ref,
    down_lands,
    down_across_ref,
    up_lands,
    up_across_ref,
    qkv_lands,
    qkv_across_ref,
    norm_ref,
    norm_land_ref,
    q_ref,
    k_ref,
    v_ref,
    qt_ref,
    kt_ref,
    xt_ref,
    ot_ref,
    lse_ref,
    results_ref,
    stage_ref,
    key_marks_ref,
    query_marks_ref,
    own_seg_ref,
    seg_line_ref,
    send_sem,
    recv_sem,
    local_sem,
):
    tensors, rows, width = x_col_ref.shape
    owners = tensors // columns
    lanes = mixed_ref.shape[-1]
    heads = lanes // E
    pairs = heads // 2
    share = all_up_ref.shape[-1]
    shard = width // tensors
    last = tensors - 1
    length = tensors * rows
    tokens = columns * rows
    tensor_bits = log2(tensors)
    me = lax.axis_index("tensor")
    me_low = me % owners
    links = Links(send_sem, recv_sem)

    def slot_copies(sources, land):
        first = links.take(last)

        def one(slot, partner):
            source = sources.at[slot, :, pl.ds(0, land.shape[-1])]
            return links.copy(source, land.at[slot], first + slot, "tensor", partner)

        return one

    def partner_of(slot):
        mask = last - slot
        index = me
        for bit in range(log2(tensors)):
            index = index + bit_of(mask, bit) * (1 - 2 * bit_of(me, bit)) * (1 << bit)
        return index

    def gather(src, dst, lead, first, direct):
        cut_bits = len(dst.shape) - lead - 3
        return WeightGather(links, src, dst, lead, cut_bits, dp_bits, first, direct)

    masks = range(1, tensors)
    qkv = Stages([gather(None, all_qkv_ref, 1, 0, True)], masks)
    ffn = [
        gather(w_out_ref, all_out_ref, 0, 0, False),
        gather(w_up_ref, all_up_ref, 0, 0, False),
        gather(w_down_ref, all_down_ref, 0, 1, False),
    ]
    levels = [[mask for mask in masks if mask.bit_count() == n + 1] for n in range(tensor_bits)]
    near_ffn = Stages(ffn, [1])
    far_ffn = [Stages(ffn, [mask for mask in level if mask != 1]) for level in levels]
    x_first = links.take(last)

    def x_copy(slot):
        partner = partner_of(slot)
        return links.copy(
            home_ref.at[0, partner // owners], x_col_ref.at[slot], x_first + slot, "tensor", partner
        )

    mixed_copy = slot_copies(stage_ref, mixed_ref)
    do_copy = slot_copies(stage_ref, do_ref)
    input_copy = slot_copies(stage_ref, input_land_ref)
    down_scatter = GradScatter(links, g_down_ref, down_lands, down_across_ref, False)
    up_scatter = GradScatter(links, g_up_ref, up_lands, up_across_ref, False)
    qkv_scatters = [
        GradScatter(links, g_qkv_ref.at[i], [land.at[i] for land in qkv_lands], qkv_across_ref.at[i], True)
        for i in range(3)
    ]
    norm_sum = NormSum(links, norm_ref, norm_land_ref, dp_bits, tensors)

    def next_x(slot):
        x_copy(slot).wait_send()
        if slot + 1 < last - 1:
            x_copy(slot + 1).start()

    gain_one, bias_one = gain_one_ref[...], bias_one_ref[...]
    gain_two, bias_two = gain_two_ref[...], bias_two_ref[...]
    shard_copies = [one.own_copy(local_sem.at[5 + i]) for i, one in enumerate(ffn)]

    def start_phase(raw_ref, raw_qkv_ref):
        loads = [
            pltpu.make_async_copy(ref, raw_ref.at[n], local_sem.at[n])
            for n, ref in enumerate((x_ref, dual_in_ref, cot_post_ref, cot_dual_ref))
        ]
        load_qkv = pltpu.make_async_copy(w_qkv_ref, raw_qkv_ref, local_sem.at[4])
        start(loads[:1] + [load_qkv] + loads[1:] + shard_copies)
        greet(dp_bits, tensors)
        load_qkv.wait()
        for i in range(3):
            all_qkv_ref[me, i] = raw_qkv_ref[i].T.reshape(all_qkv_ref.shape[2:])
        loads[0].wait()
        home_ref[0] = jnp.swapaxes(raw_ref[0], 0, 1)
        greeted(dp_bits, tensors)
        qkv.begin()
        x_copy(0).start()
        if last > 1:
            x_copy(last - 1).start()
        near_ffn.begin()
        x_col_ref[last] = home_ref[0, me // owners]
        norm_ref[...] = jnp.zeros_like(norm_ref)
        own_seg_ref[...] = jnp.zeros_like(own_seg_ref)
        seg_row = lax.broadcasted_iota(jnp.int32, seg_ref.shape, 0)
        own_seg = jnp.where(seg_row == me // owners, seg_ref[...], 0).astype(F32)
        seg_line_ref[0:1, :] = jnp.sum(own_seg, axis=0, keepdims=True)
        for slot in range(tensors):
            spot = pl.ds(pl.multiple_of(partner_of(slot) * rows, rows), rows)
            own_seg_ref[slot : slot + 1, :] = seg_line_ref[0:1, spot]
        seg_columns = own_seg_ref[...].T
        for slot in range(tensors):
            at = slice(slot * rows, (slot + 1) * rows)
            lane = lax.broadcasted_iota(jnp.int32, (rows, 2 * E), 1)
            same = seg_columns[:, slot : slot + 1] == lane.astype(F32)
            marks = jnp.where(lane < DOCUMENTS, same.astype(F32), 0.0)
            ones = jnp.where((lane >= DOCUMENTS) & (lane < DOCUMENTS + PARTS), 1.0, marks)
            key_marks_ref[at, :] = ones.astype(BF16)
            line = lax.broadcasted_iota(jnp.int32, (2 * E, rows), 0)
            other = own_seg_ref[slot : slot + 1, :] != line.astype(F32)
            bias = jnp.where((line < DOCUMENTS) & other, NEGATIVE, 0.0)
            query_marks_ref[:, at] = bias.astype(BF16)
        if owners > 1:
            g_qkv_ref[...] = jnp.zeros_like(g_qkv_ref)
        turned = 1
        for stage in range(qkv.count):
            if turned < 4:
                loads[turned].wait()
                home_ref[turned] = jnp.swapaxes(raw_ref[turned], 0, 1)
                turned += 1
            if stage == qkv.count - 1:
                next_x(0)
                near_ffn.advance(0)
            qkv.advance(stage)
        for copy in shard_copies:
            copy.wait()

    pl.run_scoped(
        start_phase,
        pltpu.VMEM((4, rows, columns, width), BF16),
        pltpu.VMEM(w_qkv_ref.shape, BF16),
    )
    own_shards = pl.ds(me_low * (tensors // owners), tensors // owners)

    def w_t(i):
        return all_qkv_ref[own_shards, i].reshape(lanes, width)

    def forward_phase(
        vt_ref,
        hidden_ref,
        slope_ref,
        grad_inner_ref,
        up_two_ref,
        middle_ref,
        up_one_ref,
    ):
        order = [last, last - 1] + list(range(last - 1)) if last > 1 else [last, 0]
        for turn, slot in enumerate(order):
            if slot < last:
                x_copy(slot).wait_recv()
            if 0 < slot < last - 1:
                next_x(slot)
            if turn + 1 == tensors:
                far_ffn[0].begin()
            block = x_col_ref[slot]
            at = slice(slot * rows, (slot + 1) * rows)
            q_ref[at, :] = dot_nt(block, w_t(0)).astype(BF16) * jnp.bfloat16(0.125)
            k_ref[at, :] = dot_nt(block, w_t(1)).astype(BF16)
            v_ref[at, :] = dot_nt(block, w_t(2)).astype(BF16)
            qt_ref[:, at] = dot_nt(w_t(0), block).astype(BF16) * jnp.bfloat16(0.125)
            kt_ref[:, at] = dot_nt(w_t(1), block).astype(BF16)
            vt_ref[:, at] = dot_nt(w_t(2), block).astype(BF16)
            xt_ref[:, at] = block.T
            if 0 < turn < near_ffn.count:
                near_ffn.advance(turn)
        for stage in range(tensors, near_ffn.count):
            near_ffn.advance(stage)

        def gather_step(level, stage):
            def run():
                far_ffn[level].advance(stage)
                if stage == 0 and level + 1 < len(far_ffn):
                    far_ffn[level + 1].begin()

            return run

        steps = tensors * pairs
        gather_events = sorted(
            (
                (GATHER_DUE + GATHER_LEVEL * level + GATHER_STEP * stage, level, stage)
                for level in range(tensor_bits)
                for stage in range(1 + dp_bits)
            ),
        )
        late = [gather_step(*which) for due, *which in gather_events if due >= 16]
        gather_events = [
            (due * steps // 16, gather_step(*which)) for due, *which in gather_events if due < 16
        ]

        @pl.loop(0, tensors)
        def _(slot):
            at_rows = pl.ds(pl.multiple_of(slot * rows, rows), rows)
            @pl.loop(0, pairs)
            def _(j):
                for due, one in gather_events:

                    @pl.when(slot * pairs + j == due)
                    def _():
                        one()

                at = pl.ds(pl.multiple_of(j * 2 * E, 2 * E), 2 * E)
                keys = jnp.concatenate([k_ref[:, at], key_marks_ref[...]], axis=1)
                queries = qt_ref[at, at_rows]
                marks = query_marks_ref[:, at_rows]
                for half in range(2):
                    scores = dot_nn(keys, with_marks(half_rows(queries, half), marks))
                    top = jnp.max(scores, axis=0, keepdims=True)
                    raised = jnp.exp(scores - top)
                    denom = jnp.sum(raised, axis=0, keepdims=True)
                    at_head = pl.ds(pl.multiple_of((2 * j + half) * E, E), E)
                    result = dot_nn(vt_ref[at_head, :], raised.astype(BF16))
                    ot_ref[slot, at_head, :] = result * (1.0 / denom)
                    lse_ref[slot, pl.ds(2 * j + half, 1), :] = top + jnp.log(denom)

            block = ot_ref[slot].T.astype(BF16)

            @pl.when(slot < last)
            def _():
                stage_ref[slot, :, :lanes] = block
                mixed_copy(slot, partner_of(slot)).start()

            @pl.when(slot == last)
            def _():
                mixed_ref[last] = block

        for one in late:
            one()

        @pl.loop(0, columns)
        def _(i):
            column = partner_of(owners * i) // owners
            for r in range(owners):

                @pl.when(owners * i + r < last)
                def _():
                    mixed_copy(owners * i + r, partner_of(owners * i + r)).wait()

            def slot_of(h):
                return last - owners * (columns - 1 - i) - flip(me_low, h)

            mixed = jnp.concatenate([mixed_ref[slot_of(h)] for h in range(owners)], axis=1)
            at = pl.ds(pl.multiple_of(i * rows, rows), rows)
            branch_one = dot_nn(mixed, all_out_ref[...].reshape(width, width))
            normed_one, factor_one = norm_forward(home_ref[0, column].astype(F32) + branch_one)
            middle = normed_one * gain_one + bias_one
            middle_low = middle.astype(BF16)
            middle_ref[:, at] = middle_low.T
            branch_two = jnp.zeros((rows, width), F32)

            for t in range(tensors):
                inner = dot_nn(middle_low, all_up_ref[t].reshape(width, share))
                square = inner * inner
                bend = jnp.tanh(GELU_A * (inner + GELU_B * (square * inner)))
                hidden = (0.5 * inner * (1.0 + bend)).astype(BF16)
                slope_ref[t] = 0.5 * (1.0 + bend) + (0.5 * GELU_A) * inner * (
                    1.0 - bend * bend
                ) * (1.0 + (3.0 * GELU_B) * square)
                hidden_ref[t, at, :] = hidden
                branch_two = branch_two + dot_nn(hidden, all_down_ref[t].reshape(share, width))
            normed_two, factor_two = norm_forward(middle + branch_two)
            results_ref[0, column] = normed_two * gain_two + bias_two
            results_ref[1, column] = home_ref[1, column].astype(F32) + branch_one + branch_two
            cot_dual = home_ref[3, column].astype(F32)
            upstream = home_ref[2, column].astype(F32)
            d_two = norm_backward(upstream, normed_two, factor_two, gain_two)
            norm_ref[2:3, :] += jnp.sum(upstream * normed_two, axis=0, keepdims=True)
            norm_ref[3:4, :] += jnp.sum(upstream, axis=0, keepdims=True)
            up_two = (d_two + cot_dual).astype(BF16)
            up_two_ref[:, at] = up_two.T
            grad_middle = d_two
            for t in range(tensors):
                grad_hidden = dot_nt(up_two, all_down_ref[t].reshape(share, width))
                grad_inner = (grad_hidden * slope_ref[t]).astype(BF16)
                grad_inner_ref[t, at, :] = grad_inner
                grad_middle = grad_middle + dot_nt(grad_inner, all_up_ref[t].reshape(width, share))
            d_one = norm_backward(grad_middle, normed_one, factor_one, gain_one)
            norm_ref[0:1, :] += jnp.sum(grad_middle * normed_one, axis=0, keepdims=True)
            norm_ref[1:2, :] += jnp.sum(grad_middle, axis=0, keepdims=True)
            results_ref[2, column] = d_one
            up_one = (d_one + cot_dual).astype(BF16)
            up_one_ref[:, at] = up_one.T
            grad_mixed = dot_nt(up_one, all_out_ref[...].reshape(width, width)).astype(BF16)
            for h in range(owners):
                slot = slot_of(h)
                piece = grad_mixed[:, h * lanes : (h + 1) * lanes]

                @pl.when(slot < last)
                def _():
                    stage_ref[slot, :, :lanes] = piece
                    do_copy(slot, partner_of(slot)).start()

                @pl.when(slot == last)
                def _():
                    do_ref[last] = piece

        norm_sum.begin()
        cut = (2,) * dp_bits + (width >> dp_bits,)

        @pl.loop(0, tensors)
        def _(t):
            g_down = dot_nn(up_two_ref[...], hidden_ref[t]).astype(BF16)
            g_down_ref[t] = g_down.reshape(cut + (share,))

        down_scatter.begin()
        every = (slice(None),) * (dp_bits + 1)

        @pl.loop(0, tensors)
        def _(t):
            g_up = dot_nn(middle_ref[...], grad_inner_ref[t]).astype(BF16)
            g_up_ref[(t,) + every + (slice(0, share),)] = g_up.reshape(cut + (share,))

        def mixed_of(i):
            def slot_of(h):
                return last - owners * (columns - 1 - i) - flip(me_low, h)

            return jnp.concatenate([mixed_ref[slot_of(h)] for h in range(owners)], axis=1)

        all_mixed = jnp.concatenate([mixed_of(i) for i in range(columns)], axis=0)
        g_out = dot_nn(up_one_ref[...], all_mixed).astype(BF16)
        for t in range(tensors):
            g_up_ref[(t,) + every + (slice(share, share + shard),)] = g_out[
                :, t * shard : (t + 1) * shard
            ].reshape(cut + (shard,))
        up_scatter.begin()

    pl.run_scoped(
        forward_phase,
        pltpu.VMEM((lanes, length), BF16),
        pltpu.VMEM((tensors, tokens, share), BF16),
        pltpu.VMEM((tensors, rows, share), F32),
        pltpu.VMEM((tensors, tokens, share), BF16),
        pltpu.VMEM((width, tokens), BF16),
        pltpu.VMEM((width, tokens), BF16),
        pltpu.VMEM((width, tokens), BF16),
    )

    def backward_phase(dot_ref, delta_ref, dq_ref, dk_ref, dv_ref, grads_ref):
        dq_ref[...] = jnp.zeros_like(dq_ref)
        dk_ref[...] = jnp.zeros_like(dk_ref)
        dv_ref[...] = jnp.zeros_like(dv_ref)

        def receive(slot):
            if slot < last:
                do_copy(slot, partner_of(slot)).wait()
            at = slice(slot * rows, (slot + 1) * rows)
            turned = do_ref[slot].T
            dot_ref[:, at] = turned
            product = turned.astype(F32) * ot_ref[slot]
            delta_ref[slot, :heads] = jnp.sum(product.reshape(heads, E, rows), axis=1)

        def advance(scatter, step):
            def run():
                scatter.advance(step)
                if scatter is up_scatter:
                    norm_sum.advance(step)

            return run

        counts = [
            count for wave in range(tensors) for count in (tensors - wave, last - wave) if count
        ]
        begins, done = [], 0
        for count in counts:
            for j in range(pairs):
                begins.append((done + count * j / pairs) / (tensors * tensors))
            done += count
        count = down_scatter.steps
        wishes = []
        for scatter, dues in ((down_scatter, DOWN_DUES), (up_scatter, UP_DUES)):
            wishes.append((dues[0], advance(scatter, 0)))
            for step in range(1, count):
                due = dues[1] + (dues[2] - dues[1]) * (step - 1) / max(count - 2, 1)
                wishes.append((due, advance(scatter, step)))
        wishes = [(next(n for n, at in enumerate(begins) if at >= wish), one) for wish, one in wishes]

        def block_of(number, q_slot, q_count, k_slot, k_count):
            at_q = slice(q_slot * rows, (q_slot + q_count) * rows)
            at_k = slice(k_slot * rows, (k_slot + k_count) * rows)

            @pl.loop(0, pairs)
            def _(j):
                for place, one in wishes:
                    if place // pairs == number:

                        @pl.when(j == place % pairs)
                        def _():
                            one()

                at = pl.ds(pl.multiple_of(j * 2 * E, 2 * E), 2 * E)
                key_marks = key_marks_ref[at_k, :]
                keys = jnp.concatenate([k_ref[at_k, at], key_marks], axis=1)
                values = jnp.concatenate([v_ref[at_k, at], key_marks], axis=1)
                query_marks = query_marks_ref[:, at_q]
                no_marks = jnp.zeros_like(query_marks)
                queries = q_ref[at_q, at]
                ups = do_ref[q_slot : q_slot + q_count, :, at].reshape(q_count * rows, 2 * E)
                sums = []
                for half in range(2):

                    def row_of(ref):
                        row = pl.ds(2 * j + half, 1)
                        slots = range(q_slot, q_slot + q_count)
                        return jnp.concatenate([ref[slot, row, :] for slot in slots], axis=1)

                    minus_lse = with_row(query_marks, row_of(lse_ref))
                    minus_delta = with_row(no_marks, row_of(delta_ref))
                    probs = jnp.exp(dot_nn(keys, with_marks(half_rows(qt_ref[at, at_q], half), minus_lse)))
                    pushed = dot_nn(values, with_marks(half_rows(dot_ref[at, at_q], half), minus_delta))
                    delta = (probs * pushed).astype(BF16)
                    at_head = pl.ds(pl.multiple_of((2 * j + half) * E, E), E)
                    dq_ref[at_head, at_q] += dot_nn(kt_ref[at_head, at_k], delta)
                    sums.append((dot_nn(delta, queries), dot_nn(probs.astype(BF16), ups)))
                low_half = lax.broadcasted_iota(jnp.int32, sums[0][0].shape, 1) < E
                dk_ref[at_k, at] += jnp.where(low_half, sums[0][0], sums[1][0])
                dv_ref[at_k, at] += jnp.where(low_half, sums[0][1], sums[1][1])

        for wave in range(tensors):
            if wave == 0:
                receive(0)
            block_of(2 * wave, wave, 1, wave, tensors - wave)
            if wave == 0:
                for slot in range(1, tensors):
                    receive(slot)
            if wave < last:
                block_of(2 * wave + 1, wave + 1, last - wave, wave, 1)
            at = slice(wave * rows, (wave + 1) * rows)
            grads = (
                (dq_ref[:, at] * 0.125).T.astype(BF16),
                dk_ref[at, :].astype(BF16),
                dv_ref[at, :].astype(BF16),
            )
            part = jnp.zeros((rows, width), F32)
            for i in range(3):
                grads_ref[i, at, :] = grads[i]
                part = part + dot_nn(grads[i], w_t(i))

            if wave < last:
                stage_ref[wave] = part.astype(BF16)
                input_copy(wave, partner_of(wave)).start()
            else:
                results_ref[2, me // owners] += part

        for i in range(3):
            g = dot_nn(xt_ref[...], grads_ref[i]).astype(BF16)
            for t in range(tensors // owners):
                g_qkv_ref[i, me_low * (tensors // owners) + t] = g[
                    :, t * shard : (t + 1) * shard
                ].reshape((2,) * dp_bits + (width >> dp_bits, shard))
            qkv_scatters[i].begin()
            if i:
                qkv_scatters[i - 1].advance(0)

    pl.run_scoped(
        backward_phase,
        pltpu.VMEM((lanes, length), BF16),
        pltpu.VMEM((tensors, max(heads, 8), rows), F32),
        pltpu.VMEM((lanes, length), F32),
        pltpu.VMEM((length, lanes), F32),
        pltpu.VMEM((length, lanes), F32),
        pltpu.VMEM((3, length, lanes), BF16),
    )


    def end_phase(turned_ref):
        stores = [
            pltpu.make_async_copy(turned_ref.at[n], ref, local_sem.at[n])
            for n, ref in enumerate((post_ref, dual_ref, grad_post_ref))
        ]

        def store(n):
            turned_ref[n] = jnp.swapaxes(results_ref[n], 0, 1)
            stores[n].start()

        def advance(step):
            for one in qkv_scatters:
                one.advance(step)

        store(0)
        qkv_scatters[2].advance(0)
        store(1)
        if dp_bits > 1:
            advance(1)
        if last > 1:
            x_copy(last - 1).wait_send()
        for slot in range(last):
            input_copy(slot, partner_of(slot)).wait()
            results_ref[2, partner_of(slot) // owners] += input_land_ref[slot].astype(F32)
        store(2)
        for step in range(2, dp_bits):
            advance(step)
        r_down_ref[...] = down_scatter.result()
        r_up_ref[...] = up_scatter.result()
        count = width // (tensors << dp_bits)
        first = (lax.axis_index("dp") * tensors + me) * count
        r_norm_ref[...] = pltpu.roll(norm_sum.result(), width - first, 1)[:, : r_norm_ref.shape[1]]
        for i in range(3):
            r_qkv_ref[i] = qkv_scatters[i].result()
        for copy in stores:
            copy.wait()

    pl.run_scoped(end_phase, pltpu.VMEM((3, rows, columns, width), F32))


def hand_over_kernel(*refs):
    sources, results = refs[:7], refs[7:]
    for n in range(3):
        results[n][...] = sources[n][...]

    @pl.when(pl.program_id(0) == 0)
    def _():
        grad_qkv, grad_down, grad_up_out, grad_norm = sources[3:]
        share = results[4].shape[1]
        results[3][...] = grad_qkv[...]
        results[4][...] = grad_down[...]
        results[5][...] = grad_up_out[:, :share]
        results[6][...] = grad_up_out[:, share:]
        for n in range(4):
            results[7 + n][...] = grad_norm[n : n + 1, : results[7 + n].shape[1]]


def body(
    x_post,
    x_dual,
    cot_post,
    cot_dual,
    segment_ids,
    w_qkv,
    w_out,
    w_up,
    w_down,
    gain_one,
    bias_one,
    gain_two,
    bias_two,
):
    tensors, devices = lax.axis_size("tensor"), lax.axis_size("dp")
    dp_bits = log2(devices)
    rows, columns, width = x_post.shape
    length = tensors * rows
    owners = tensors // columns
    lanes = width // owners
    share, shard = w_up.shape[1], w_out.shape[0]
    piece = width // devices
    heads = lanes // E
    me = lax.axis_index("tensor")
    def cut(array, dim):
        bits = min(dp_bits, log2(array.shape[dim] // 16))
        shape = array.shape[:dim] + (2,) * bits + (array.shape[dim] >> bits,) + array.shape[dim + 1 :]
        return array.reshape(shape)

    shards = [cut(w_out, 0), cut(w_up, 0), cut(w_down, 0)]
    qkv_shape = jax.eval_shape(lambda w: cut(jnp.swapaxes(w, 1, 2), 1), w_qkv).shape
    in_vmem = pl.BlockSpec(memory_space=pltpu.VMEM)
    in_place = pl.BlockSpec(memory_space=pl.ANY)
    shape = jax.ShapeDtypeStruct
    bits = (2,) * dp_bits

    def lands(lane_count, *lead):
        return [
            pltpu.VMEM(lead + (tensors,) + bits[: dp_bits - 1 - step] + (piece, lane_count), BF16)
            for step in range(dp_bits)
        ]

    layer = pl.pallas_call(
        functools.partial(layer_kernel, dp_bits, columns),
        out_shape=(
            shape((rows, columns, width), F32),
            shape((rows, columns, width), F32),
            shape((rows, columns, width), F32),
            shape((3, piece, shard), F32),
            shape((piece, share), F32),
            shape((piece, share + shard), F32),
            shape((8, 128), F32),
        ),
        in_specs=[in_vmem] + [in_place] * 8 + [in_vmem] * 4,
        out_specs=(in_place,) * 3 + (in_vmem,) * 4,
        scratch_shapes=[
            pltpu.VMEM((4, columns, rows, width), BF16),
            pltpu.VMEM((tensors, rows, width), BF16),
            pltpu.VMEM((tensors,) + qkv_shape, BF16),
        ]
        + [pltpu.VMEM((tensors,) + one.shape, BF16) for one in shards]
        + [
            pltpu.VMEM((tensors, rows, lanes), BF16),
            pltpu.VMEM((tensors, rows, lanes), BF16),
            pltpu.VMEM((tensors - 1, rows, width), BF16),
            pltpu.VMEM((tensors,) + bits + (piece, share), BF16),
            pltpu.VMEM((tensors,) + bits + (piece, share + shard), BF16),
            pltpu.VMEM((3, tensors) + bits + (piece, shard), BF16),
            lands(share),
            pltpu.VMEM((tensors - 1, piece, share), BF16),
            lands(share + shard),
            pltpu.VMEM((tensors - 1, piece, share + shard), BF16),
            lands(shard, 3),
            pltpu.VMEM((3, tensors - 1, piece, shard), BF16),
            pltpu.VMEM((8, width), F32),
            pltpu.VMEM((dp_bits + tensors - 1, 8, width), F32),
            pltpu.VMEM((length, lanes), BF16),
            pltpu.VMEM((length, lanes), BF16),
            pltpu.VMEM((length, lanes), BF16),
            pltpu.VMEM((lanes, length), BF16),
            pltpu.VMEM((lanes, length), BF16),
            pltpu.VMEM((width, length), BF16),
            pltpu.VMEM((tensors, lanes, rows), F32),
            pltpu.VMEM((tensors, max(heads, 8), rows), F32),
            pltpu.VMEM((3, columns, rows, width), F32),
            pltpu.VMEM((tensors - 1, rows, width), BF16),
            pltpu.VMEM((length, 2 * E), BF16),
            pltpu.VMEM((2 * E, length), BF16),
            pltpu.VMEM((max(tensors, 8), rows), F32),
            pltpu.VMEM((8, length), F32),
            pltpu.SemaphoreType.DMA((LINKS,)),
            pltpu.SemaphoreType.DMA((LINKS,)),
            pltpu.SemaphoreType.DMA((8,)),
        ],
        compiler_params=pltpu.CompilerParams(
            vmem_limit_bytes=VMEM_BYTES, collective_id=0, has_side_effects=True
        ),
        name="layer",
    )
    made = layer(
        segment_ids.T,
        x_post,
        x_dual,
        cot_post,
        cot_dual,
        w_qkv,
        *shards,
        *(one.reshape(1, width) for one in (gain_one, bias_one, gain_two, bias_two)),
    )
    count = width // (tensors * devices)
    blocks = 2
    block_spec = pl.BlockSpec((rows // blocks, columns, width), lambda i: (i, 0, 0))

    def whole_spec(one):
        return pl.BlockSpec(one.shape, lambda i: (0,) * len(one.shape))

    small = (
        shape((3, piece, shard), F32),
        shape((piece, share), F32),
        shape((piece, share), F32),
        shape((piece, shard), F32),
    ) + (shape((1, count), F32),) * 4
    results = pl.pallas_call(
        hand_over_kernel,
        out_shape=tuple(shape(one.shape, F32) for one in made[:3]) + small,
        grid=(blocks,),
        in_specs=[block_spec] * 3 + [whole_spec(one) for one in made[3:]],
        out_specs=(block_spec,) * 3 + tuple(whole_spec(one) for one in small),
        name="hand_over",
    )(*made)
    post_out, dual_out, grad_post, g_qkv, g_down, g_up, g_out = results[:7]
    norms = tuple(one.reshape(count) for one in results[7:])
    return (post_out, dual_out, grad_post, g_qkv, g_out.T, g_up, g_down.T) + norms


def solution(mesh):
    placed = (
        P("tensor", "dp", None),
        P("tensor", "dp", None),
        P("tensor", "dp", None),
        P("tensor", "dp", None),
        P(None, "dp"),
        P(None, None, "tensor"),
        P("tensor", None),
        P(None, "tensor"),
        P("tensor", None),
        P(),
        P(),
        P(),
        P(),
    )
    return jax.shard_map(
        body,
        mesh=mesh,
        in_specs=placed,
        out_specs=(
            P("tensor", "dp", None),
            P("tensor", "dp", None),
            P("tensor", "dp", None),
            P(None, "dp", "tensor"),
            P("tensor", "dp"),
            P("dp", "tensor"),
            P("tensor", "dp"),
            P(("dp", "tensor")),
            P(("dp", "tensor")),
            P(("dp", "tensor")),
            P(("dp", "tensor")),
        ),
        check_vma=False,
    )
```

time: 226 us -> 161 us (0.71)
  Pallas kernels: 202 us -> 160 us
  local copies, waits for them, and re-layouts: 21.4 us -> 0 us
    pallas_call x1 -> x2, Pallas kernels: 202 us -> 160 us  [the longest x1 155 us: body(): layer(segment_ids.T, x_post, x_dual, cot_post, cot_dual, w_qkv, *shards,...]
    unnamed x18 -> x0, local copies, waits for them, and re-layouts: 11 us -> none
    transpose x5 -> x0, local copies, waits for them, and re-layouts: 8.43 us -> none  [the longest x1 3.42 us: body(): jnp.swapaxes(x_dual, 0, 1)]
where the time goes in v3:
time: 161 us
  Pallas kernels  160 us (99%)
    pallas_call x1, Pallas kernels, body(): layer(segment_ids.T, x_post, x_dual, cot_post, cot_dual, w_qkv, *shards,...  155 us
    pallas_call x1, Pallas kernels, body(): pl.pallas_call(hand_over_kernel, out_shape=tuple((shape(one.shape, F32) f...  5.3 us

profile of v3, /device:TPU:0, one launch (start us, length us, event | category | flops | bytes accessed | tf_op | source)
XLA Modules:
  0.0 161.2 jit_solution(10217710851964830443)
XLA Ops:
  0.6 155.0 %layer.1 = (f32[256,4,512]{2,1,0:T(4,128)}, f32[256,4,512]{2,1,0:T(4,128)}, f32[256,4,512]{2,1,0:T(4,128)}, f32[3,64,128]{2,1,0:T(8,128)}, f32[64,512]{1,0:T(8,1...) custom-call(s32[4,1024]{1,0:T(4,128)} %bitcast.17, bf16[256,4,512]{2,1,0:T(4,128)(2,1)} %x_ref.1, ...), custom_call_target="tpu_custom_call" | custom-call | tf_op jit(solution)/shard_map/layer/pallas_call | solution.py:1040
  155.7 5.3 %hand_over.1 = (f32[256,4,512]{2,1,0:T(4,128)}, f32[256,4,512]{2,1,0:T(4,128)}, f32[256,4,512]{2,1,0:T(4,128)}, f32[3,64,128]{2,1,0:T(8,128)}, f32[64,512]{1,0:T...) custom-call(f32[256,4,512]{2,1,0:T(4,128)} %get-tuple-element.29.ref, ...), custom_call_target="tpu_custom_call" | custom-call | tf_op jit(solution)/shard_map/hand_over/pallas_call | solution.py:1063

commit v4 on v3

--- a/solution.py
+++ b/solution.py
@@ -15,13 +15,13 @@
 DOWN_DUES = (0.06, 0.35, 0.75)
 UP_DUES = (0.10, 0.5, 0.9)
 GATHER_DUE, GATHER_LEVEL, GATHER_STEP = 6, 4, 3
+NEAR_DUE = 1
 PARTS = 3
 GELU_A = 0.7978845608028654
 GELU_B = 0.044715
 F32 = jnp.float32
 BF16 = jnp.bfloat16
 VMEM_BYTES = 63 * 1024 * 1024
-LINKS = 320
 
 
 def dot_nn(a, b):
@@ -94,23 +94,51 @@
 
 class Links:
     def __init__(self, send_sem, recv_sem):
-        self.send_sem, self.recv_sem, self.used = send_sem, recv_sem, 0
+        self.send_sem, self.recv_sem, self.used, self.pooled = send_sem, recv_sem, 0, 0
 
     def take(self, count):
         first = self.used
         self.used += count
-        assert self.used <= self.send_sem.shape[0]
+        assert self.used <= self.recv_sem.shape[0]
         return first
 
-    def copy(self, src, dst, slot, axis, partner):
+    def pool(self, count):
+        first = self.pooled
+        self.pooled += count
+        assert self.pooled <= self.send_sem.shape[0]
+        return first
+
+    def copy(self, src, dst, slot, send_slot, axis, partner):
         return pltpu.make_async_remote_copy(
             src_ref=src,
             dst_ref=dst,
-            send_sem=self.send_sem.at[slot],
+            send_sem=self.send_sem.at[send_slot],
             recv_sem=self.recv_sem.at[slot],
             device_id={axis: partner},
             device_id_type=MESH,
         )
+
+    def stages(self, stages):
+        first = self.pool(max(len(stage) for stage in stages))
+        return [
+            [
+                self.copy(src, dst, self.take(1), first + n, axis, partner)
+                for n, (src, dst, axis, partner) in enumerate(stage)
+            ]
+            for stage in stages
+        ]
+
+
+def link_counts(tensors, dp_bits, cuts):
+    others = tensors - 1
+    levels = [0] * log2(tensors)
+    for mask in range(2, tensors):
+        levels[mask.bit_count() - 1] += 1
+    receive = 4 * others + others * (1 + 3 * cuts[0]) + sum(others * (1 + cut) for cut in cuts[1:])
+    receive += 5 * (1 + 2 * (dp_bits - 1) + others) + dp_bits + others
+    send = 2 * others + 3 * others + 3 + 3 * sum(levels)
+    send += 2 * max(2, tensors // 2) + 3 * max(2, others) + others
+    return receive, send
 
 
 def start(copies):
@@ -140,7 +168,7 @@
 
 
 class WeightGather:
-    def __init__(self, links, src, dst, lead, cut_bits, dp_bits, first, direct):
+    def __init__(self, src, dst, lead, cut_bits, dp_bits, first, direct=False):
         tensors = dst.shape[0]
         dp, me = lax.axis_index("dp"), lax.axis_index("tensor")
         bits = list(range(dp_bits - 1, dp_bits - 1 - cut_bits, -1))
@@ -159,10 +187,9 @@
             block = flip(me, mask - near)
             stages = [[] for _ in range(1 + dp_bits)]
             stages[0].append(
-                links.copy(
+                (
                     dst.at[(block,) + piece] if mask != near else src.at[piece],
                     dst.at[(block,) + piece],
-                    links.take(1),
                     "tensor",
                     flip(me, near),
                 )
@@ -177,13 +204,7 @@
                         slice(None) if other in done else bit_of(dp, other) for other in bits
                     )
                     stages[1 + phase].append(
-                        links.copy(
-                            dst.at[region],
-                            dst.at[region],
-                            links.take(1),
-                            "dp",
-                            flip(dp, 1 << bit),
-                        )
+                        (dst.at[region], dst.at[region], "dp", flip(dp, 1 << bit))
                     )
             self.stages[mask] = stages
 
@@ -192,13 +213,9 @@
 
 
 class Stages:
-    def __init__(self, weights, masks):
-        count = len(weights[0].stages[masks[0]])
-        self.copies = [
-            [copy for one in weights for mask in masks for copy in one.stages[mask][stage]]
-            for stage in range(count)
-        ]
-        self.count = count
+    def __init__(self, links, stages):
+        self.copies = links.stages(stages)
+        self.count = len(stages)
 
     def begin(self):
         start(self.copies[0])
@@ -207,6 +224,14 @@
         finish(self.copies[stage])
         if stage + 1 < self.count:
             start(self.copies[stage + 1])
+
+
+def shard_stages(weights, masks):
+    count = len(weights[0].stages[masks[0]])
+    return [
+        [copy for one in weights for mask in masks for copy in one.stages[mask][stage]]
+        for stage in range(count)
+    ]
 
 
 class GradScatter:
@@ -217,13 +242,11 @@
         dp_bits = len(lands)
         high = list(range(dp_bits - 1, 0, -1))
         middle = self.tensors // 2
-        first = links.take(1)
         copies = [
             [
-                links.copy(
+                (
                     grad.at[(slice(None),) * dp_bits + (1 - bit_of(self.dp, 0),)],
                     lands[0],
-                    first,
                     "dp",
                     flip(self.dp, 1),
                 )
@@ -241,10 +264,9 @@
                 part = pl.ds(begin, middle)
                 index = (part,) + (slice(None),) * place + (1 - bit_of(self.dp, bit),)
                 copies[step].append(
-                    links.copy(
+                    (
                         lands[step - 1].at[index],
                         lands[step].at[part],
-                        links.take(1),
                         "dp",
                         flip(self.dp, 1 << bit),
                     )
@@ -259,10 +281,9 @@
             for high in range(self.tensors >> (bit + 1)):
                 mask = high * 2 * step
                 found.append(
-                    links.copy(
+                    (
                         lands[-1].at[flip(self.me, mask + step)],
                         across.at[place],
-                        links.take(1),
                         "tensor",
                         flip(self.me, step),
                     )
@@ -274,10 +295,9 @@
         if direct:
             copies.append(
                 [
-                    links.copy(
+                    (
                         lands[-1].at[flip(self.me, step)],
                         across.at[step - 1],
-                        links.take(1),
                         "tensor",
                         flip(self.me, step),
                     )
@@ -285,7 +305,8 @@
                 ]
             )
             self.joins = [[(0, step) for step in range(self.tensors - 1)]]
-        self.copies, self.sums = copies, sums + [[] for _ in self.joins[1:]]
+        self.copies = links.stages(copies)
+        self.sums = sums + [[] for _ in self.joins[1:]]
         self.steps = len(copies) - 1
 
     def begin(self):
@@ -321,22 +342,16 @@
     def __init__(self, links, total, land, dp_bits, tensors):
         dp, me = lax.axis_index("dp"), lax.axis_index("tensor")
         self.total, self.land = total, land
-        self.copies = [
-            [links.copy(total, land.at[bit], links.take(1), "dp", flip(dp, 1 << bit))]
-            for bit in range(dp_bits)
+        copies = [
+            [(total, land.at[bit], "dp", flip(dp, 1 << bit))] for bit in range(dp_bits)
         ]
-        self.copies.append(
+        copies.append(
             [
-                links.copy(
-                    total,
-                    land.at[dp_bits + step - 1],
-                    links.take(1),
-                    "tensor",
-                    (me + step) % tensors,
-                )
+                (total, land.at[dp_bits + step - 1], "tensor", flip(me, step))
                 for step in range(1, tensors)
             ]
         )
+        self.copies = links.stages(copies)
 
     def begin(self):
         start(self.copies[0])
@@ -404,14 +419,20 @@
     qt_ref,
     kt_ref,
     xt_ref,
-    ot_ref,
+    o_ref,
     lse_ref,
     results_ref,
     stage_ref,
     key_marks_ref,
+    key_marks_t_ref,
     query_marks_ref,
+    query_marks_n_ref,
+    lse_columns_ref,
     own_seg_ref,
     seg_line_ref,
+    seg_in_ref,
+    norms_ref,
+    small_refs,
     send_sem,
     recv_sem,
     local_sem,
@@ -431,12 +452,16 @@
     me_low = me % owners
     links = Links(send_sem, recv_sem)
 
+    exchange_pool = links.pool(last)
+
     def slot_copies(sources, land):
         first = links.take(last)
 
         def one(slot, partner):
             source = sources.at[slot, :, pl.ds(0, land.shape[-1])]
-            return links.copy(source, land.at[slot], first + slot, "tensor", partner)
+            return links.copy(
+                source, land.at[slot], first + slot, exchange_pool + slot, "tensor", partner
+            )
 
         return one
 
@@ -447,26 +472,33 @@
             index = index + bit_of(mask, bit) * (1 - 2 * bit_of(me, bit)) * (1 << bit)
         return index
 
-    def gather(src, dst, lead, first, direct):
-        cut_bits = len(dst.shape) - lead - 3
-        return WeightGather(links, src, dst, lead, cut_bits, dp_bits, first, direct)
-
-    masks = range(1, tensors)
-    qkv = Stages([gather(None, all_qkv_ref, 1, 0, True)], masks)
+    def gather(src, dst, lead, first, direct=False):
+        return WeightGather(src, dst, lead, len(dst.shape) - lead - 3, dp_bits, first, direct)
+
+    masks = list(range(1, tensors))
+    levels = [[mask for mask in masks if mask.bit_count() == n + 1] for n in range(tensor_bits)]
+    qkv = Stages(links, shard_stages([gather(None, all_qkv_ref, 1, 0, True)], masks))
     ffn = [
-        gather(w_out_ref, all_out_ref, 0, 0, False),
-        gather(w_up_ref, all_up_ref, 0, 0, False),
-        gather(w_down_ref, all_down_ref, 0, 1, False),
+        gather(w_out_ref, all_out_ref, 0, 0),
+        gather(w_up_ref, all_up_ref, 0, 0),
+        gather(w_down_ref, all_down_ref, 0, 1),
     ]
-    levels = [[mask for mask in masks if mask.bit_count() == n + 1] for n in range(tensor_bits)]
-    near_ffn = Stages(ffn, [1])
-    far_ffn = [Stages(ffn, [mask for mask in level if mask != 1]) for level in levels]
+    near_ffn = Stages(links, shard_stages(ffn, [1]))
+    far_ffn = [
+        Stages(links, shard_stages(ffn, [mask for mask in level if mask != 1])) for level in levels
+    ]
+    x_pool = links.pool(last)
     x_first = links.take(last)
 
     def x_copy(slot):
         partner = partner_of(slot)
         return links.copy(
-            home_ref.at[0, partner // owners], x_col_ref.at[slot], x_first + slot, "tensor", partner
+            home_ref.at[0, partner // owners],
+            x_col_ref.at[slot],
+            x_first + slot,
+            x_pool + slot,
+            "tensor",
+            partner,
         )
 
     mixed_copy = slot_copies(stage_ref, mixed_ref)
@@ -485,8 +517,6 @@
         if slot + 1 < last - 1:
             x_copy(slot + 1).start()
 
-    gain_one, bias_one = gain_one_ref[...], bias_one_ref[...]
-    gain_two, bias_two = gain_two_ref[...], bias_two_ref[...]
     shard_copies = [one.own_copy(local_sem.at[5 + i]) for i, one in enumerate(ffn)]
 
     def start_phase(raw_ref, raw_qkv_ref):
@@ -495,7 +525,11 @@
             for n, ref in enumerate((x_ref, dual_in_ref, cot_post_ref, cot_dual_ref))
         ]
         load_qkv = pltpu.make_async_copy(w_qkv_ref, raw_qkv_ref, local_sem.at[4])
-        start(loads[:1] + [load_qkv] + loads[1:] + shard_copies)
+        small_loads = [pltpu.make_async_copy(seg_ref, seg_in_ref, local_sem.at[8])] + [
+            pltpu.make_async_copy(ref, norms_ref.at[pl.ds(n, 1)], local_sem.at[9 + n])
+            for n, ref in enumerate((gain_one_ref, bias_one_ref, gain_two_ref, bias_two_ref))
+        ]
+        start(loads[:1] + [load_qkv] + loads[1:] + small_loads + shard_copies)
         greet(dp_bits, tensors)
         load_qkv.wait()
         for i in range(3):
@@ -507,12 +541,14 @@
         x_copy(0).start()
         if last > 1:
             x_copy(last - 1).start()
-        near_ffn.begin()
         x_col_ref[last] = home_ref[0, me // owners]
         norm_ref[...] = jnp.zeros_like(norm_ref)
+        lse_columns_ref[...] = jnp.zeros_like(lse_columns_ref)
         own_seg_ref[...] = jnp.zeros_like(own_seg_ref)
-        seg_row = lax.broadcasted_iota(jnp.int32, seg_ref.shape, 0)
-        own_seg = jnp.where(seg_row == me // owners, seg_ref[...], 0).astype(F32)
+        for copy in small_loads:
+            copy.wait()
+        seg_row = lax.broadcasted_iota(jnp.int32, seg_in_ref.shape, 0)
+        own_seg = jnp.where(seg_row == me // owners, seg_in_ref[...], 0).astype(F32)
         seg_line_ref[0:1, :] = jnp.sum(own_seg, axis=0, keepdims=True)
         for slot in range(tensors):
             spot = pl.ds(pl.multiple_of(partner_of(slot) * rows, rows), rows)
@@ -525,10 +561,12 @@
             marks = jnp.where(lane < DOCUMENTS, same.astype(F32), 0.0)
             ones = jnp.where((lane >= DOCUMENTS) & (lane < DOCUMENTS + PARTS), 1.0, marks)
             key_marks_ref[at, :] = ones.astype(BF16)
+            key_marks_t_ref[:, at] = ones.T.astype(BF16)
             line = lax.broadcasted_iota(jnp.int32, (2 * E, rows), 0)
             other = own_seg_ref[slot : slot + 1, :] != line.astype(F32)
             bias = jnp.where((line < DOCUMENTS) & other, NEGATIVE, 0.0)
             query_marks_ref[:, at] = bias.astype(BF16)
+            query_marks_n_ref[at, :] = bias.T.astype(BF16)
         if owners > 1:
             g_qkv_ref[...] = jnp.zeros_like(g_qkv_ref)
         turned = 1
@@ -539,7 +577,7 @@
                 turned += 1
             if stage == qkv.count - 1:
                 next_x(0)
-                near_ffn.advance(0)
+                near_ffn.begin()
             qkv.advance(stage)
         for copy in shard_copies:
             copy.wait()
@@ -555,7 +593,6 @@
         return all_qkv_ref[own_shards, i].reshape(lanes, width)
 
     def forward_phase(
-        vt_ref,
         hidden_ref,
         slope_ref,
         grad_inner_ref,
@@ -578,12 +615,9 @@
             v_ref[at, :] = dot_nt(block, w_t(2)).astype(BF16)
             qt_ref[:, at] = dot_nt(w_t(0), block).astype(BF16) * jnp.bfloat16(0.125)
             kt_ref[:, at] = dot_nt(w_t(1), block).astype(BF16)
-            vt_ref[:, at] = dot_nt(w_t(2), block).astype(BF16)
             xt_ref[:, at] = block.T
-            if 0 < turn < near_ffn.count:
-                near_ffn.advance(turn)
-        for stage in range(tensors, near_ffn.count):
-            near_ffn.advance(stage)
+            if turn == min(2, last):
+                near_ffn.advance(0)
 
         def gather_step(level, stage):
             def run():
@@ -594,6 +628,13 @@
             return run
 
         steps = tensors * pairs
+        def near_step(stage):
+            return lambda: near_ffn.advance(stage)
+
+        near_events = [
+            (NEAR_DUE + GATHER_STEP * (stage - 1), near_step(stage))
+            for stage in range(1, near_ffn.count)
+        ]
         gather_events = sorted(
             (
                 (GATHER_DUE + GATHER_LEVEL * level + GATHER_STEP * stage, level, stage)
@@ -604,7 +645,7 @@
         late = [gather_step(*which) for due, *which in gather_events if due >= 16]
         gather_events = [
             (due * steps // 16, gather_step(*which)) for due, *which in gather_events if due < 16
-        ]
+        ] + [(due * steps // 16, one) for due, one in near_events]
 
         @pl.loop(0, tensors)
         def _(slot):
@@ -618,32 +659,47 @@
                         one()
 
                 at = pl.ds(pl.multiple_of(j * 2 * E, 2 * E), 2 * E)
-                keys = jnp.concatenate([k_ref[:, at], key_marks_ref[...]], axis=1)
-                queries = qt_ref[at, at_rows]
-                marks = query_marks_ref[:, at_rows]
+                keys = with_marks(kt_ref[at, :], key_marks_t_ref[...])
+                values = jnp.concatenate([v_ref[:, at], key_marks_ref[...]], axis=1)
+                queries = q_ref[at_rows, at]
+                marks = query_marks_n_ref[at_rows, :]
+                lane = lax.broadcasted_iota(jnp.int32, queries.shape, 1)
+                results = []
                 for half in range(2):
-                    scores = dot_nn(keys, with_marks(half_rows(queries, half), marks))
-                    top = jnp.max(scores, axis=0, keepdims=True)
-                    raised = jnp.exp(scores - top)
-                    denom = jnp.sum(raised, axis=0, keepdims=True)
-                    at_head = pl.ds(pl.multiple_of((2 * j + half) * E, E), E)
-                    result = dot_nn(vt_ref[at_head, :], raised.astype(BF16))
-                    ot_ref[slot, at_head, :] = result * (1.0 / denom)
-                    lse_ref[slot, pl.ds(2 * j + half, 1), :] = top + jnp.log(denom)
-
-            block = ot_ref[slot].T.astype(BF16)
+                    own = (lane < E) if half == 0 else (lane >= E)
+                    own_queries = jnp.where(own, queries, jnp.zeros_like(queries))
+                    scores = dot_nn(jnp.concatenate([own_queries, marks], axis=1), keys)
+                    top = jnp.max(scores, axis=1, keepdims=True)
+                    raised = jnp.exp(scores - top).astype(BF16)
+                    result = dot_nn(raised, values)
+                    denom = result[:, 2 * E + DOCUMENTS : 2 * E + DOCUMENTS + 1]
+                    results.append(result[:, : 2 * E] * (1.0 / denom))
+                    lse = top + jnp.log(denom)
+                    lse_columns_ref[...] = jnp.where(
+                        lane == 2 * j + half, lse, lse_columns_ref[...]
+                    )
+                block = jnp.where(lane < E, results[0], results[1])
+                o_ref[slot, :, at] = block
+
+                @pl.when(slot < last)
+                def _():
+                    stage_ref[slot, :, at] = block.astype(BF16)
+
+                @pl.when(slot == last)
+                def _():
+                    mixed_ref[last, :, at] = block.astype(BF16)
+
+            lse_ref[slot] = lse_columns_ref[...].T[: lse_ref.shape[1]]
 
             @pl.when(slot < last)
             def _():
-                stage_ref[slot, :, :lanes] = block
                 mixed_copy(slot, partner_of(slot)).start()
-
-            @pl.when(slot == last)
-            def _():
-                mixed_ref[last] = block
 
         for one in late:
             one()
+
+        gain_one, bias_one = norms_ref[0:1, :], norms_ref[1:2, :]
+        gain_two, bias_two = norms_ref[2:3, :], norms_ref[3:4, :]
 
         @pl.loop(0, columns)
         def _(i):
@@ -744,7 +800,6 @@
 
     pl.run_scoped(
         forward_phase,
-        pltpu.VMEM((lanes, length), BF16),
         pltpu.VMEM((tensors, tokens, share), BF16),
         pltpu.VMEM((tensors, rows, share), F32),
         pltpu.VMEM((tensors, tokens, share), BF16),
@@ -762,9 +817,8 @@
             if slot < last:
                 do_copy(slot, partner_of(slot)).wait()
             at = slice(slot * rows, (slot + 1) * rows)
-            turned = do_ref[slot].T
-            dot_ref[:, at] = turned
-            product = turned.astype(F32) * ot_ref[slot]
+            dot_ref[:, at] = do_ref[slot].T
+            product = (do_ref[slot].astype(F32) * o_ref[slot]).T
             delta_ref[slot, :heads] = jnp.sum(product.reshape(heads, E, rows), axis=1)
 
         def advance(scatter, step):
@@ -907,13 +961,21 @@
         store(2)
         for step in range(2, dp_bits):
             advance(step)
-        r_down_ref[...] = down_scatter.result()
-        r_up_ref[...] = up_scatter.result()
+        small = [
+            pltpu.make_async_copy(small_refs[n], ref, local_sem.at[8 + n])
+            for n, ref in enumerate((r_qkv_ref, r_down_ref, r_up_ref, r_norm_ref))
+        ]
+        small_refs[1][...] = down_scatter.result()
+        small_refs[2][...] = up_scatter.result()
         count = width // (tensors << dp_bits)
         first = (lax.axis_index("dp") * tensors + me) * count
-        r_norm_ref[...] = pltpu.roll(norm_sum.result(), width - first, 1)[:, : r_norm_ref.shape[1]]
+        small_refs[3][...] = pltpu.roll(norm_sum.result(), width - first, 1)[:, :128]
+        start(small[1:])
         for i in range(3):
-            r_qkv_ref[i] = qkv_scatters[i].result()
+            small_refs[0][i] = qkv_scatters[i].result()
+        small[0].start()
+        for copy in small:
+            copy.wait()
         for copy in stores:
             copy.wait()
 
@@ -969,7 +1031,6 @@
 
     shards = [cut(w_out, 0), cut(w_up, 0), cut(w_down, 0)]
     qkv_shape = jax.eval_shape(lambda w: cut(jnp.swapaxes(w, 1, 2), 1), w_qkv).shape
-    in_vmem = pl.BlockSpec(memory_space=pltpu.VMEM)
     in_place = pl.BlockSpec(memory_space=pl.ANY)
     shape = jax.ShapeDtypeStruct
     bits = (2,) * dp_bits
@@ -980,19 +1041,24 @@
             for step in range(dp_bits)
         ]
 
+    small_out = (
+        shape((3, piece, shard), F32),
+        shape((piece, share), F32),
+        shape((piece, share + shard), F32),
+        shape((8, 128), F32),
+    )
+    cuts = [len(qkv_shape) - 3] + [len(one.shape) - 2 for one in shards]
+    links = link_counts(tensors, dp_bits, cuts)
     layer = pl.pallas_call(
         functools.partial(layer_kernel, dp_bits, columns),
         out_shape=(
             shape((rows, columns, width), F32),
             shape((rows, columns, width), F32),
             shape((rows, columns, width), F32),
-            shape((3, piece, shard), F32),
-            shape((piece, share), F32),
-            shape((piece, share + shard), F32),
-            shape((8, 128), F32),
-        ),
-        in_specs=[in_vmem] + [in_place] * 8 + [in_vmem] * 4,
-        out_specs=(in_place,) * 3 + (in_vmem,) * 4,
+        )
+        + small_out,
+        in_specs=[in_place] * 13,
+        out_specs=(in_place,) * 7,
         scratch_shapes=[
             pltpu.VMEM((4, columns, rows, width), BF16),
             pltpu.VMEM((tensors, rows, width), BF16),
@@ -1020,17 +1086,23 @@
             pltpu.VMEM((lanes, length), BF16),
             pltpu.VMEM((lanes, length), BF16),
             pltpu.VMEM((width, length), BF16),
-            pltpu.VMEM((tensors, lanes, rows), F32),
+            pltpu.VMEM((tensors, rows, lanes), F32),
             pltpu.VMEM((tensors, max(heads, 8), rows), F32),
             pltpu.VMEM((3, columns, rows, width), F32),
             pltpu.VMEM((tensors - 1, rows, width), BF16),
             pltpu.VMEM((length, 2 * E), BF16),
             pltpu.VMEM((2 * E, length), BF16),
+            pltpu.VMEM((2 * E, length), BF16),
+            pltpu.VMEM((length, 2 * E), BF16),
+            pltpu.VMEM((rows, 2 * E), F32),
             pltpu.VMEM((max(tensors, 8), rows), F32),
             pltpu.VMEM((8, length), F32),
-            pltpu.SemaphoreType.DMA((LINKS,)),
-            pltpu.SemaphoreType.DMA((LINKS,)),
-            pltpu.SemaphoreType.DMA((8,)),
+            pltpu.VMEM((columns, length), jnp.int32),
+            pltpu.VMEM((8, width), F32),
+            [pltpu.VMEM(one.shape, F32) for one in small_out],
+            pltpu.SemaphoreType.DMA((links[1],)),
+            pltpu.SemaphoreType.DMA((links[0],)),
+            pltpu.SemaphoreType.DMA((16,)),
         ],
         compiler_params=pltpu.CompilerParams(
             vmem_limit_bytes=VMEM_BYTES, collective_id=0, has_side_effects=True

time: 161 us -> 152 us (0.944)
  Pallas kernels: 160 us -> 151 us
    pallas_call x1, Pallas kernels: 155 us -> 146 us  [body(): layer(segment_ids.T, x_post, x_dual, cot_post, cot_dual, w_qkv, *shards,...]
where the time goes in v4:
time: 152 us
  Pallas kernels  151 us (99%)
    pallas_call x1, Pallas kernels, body(): layer(segment_ids.T, x_post, x_dual, cot_post, cot_dual, w_qkv, *shards,...  146 us
    pallas_call x1, Pallas kernels, body(): pl.pallas_call(hand_over_kernel, out_shape=tuple((shape(one.shape, F32) f...  5.3 us

profile of v4, /device:TPU:0, one launch (start us, length us, event | category | flops | bytes accessed | tf_op | source)
XLA Modules:
  0.0 152.3 jit_solution(11658459449435405994)
XLA Ops:
  0.6 146.2 %layer.1 = (f32[256,4,512]{2,1,0:T(4,128)}, f32[256,4,512]{2,1,0:T(4,128)}, f32[256,4,512]{2,1,0:T(4,128)}, f32[3,64,128]{2,1,0:T(8,128)}, f32[64,512]{1,0:T(8,1...) custom-call(s32[4,1024]{1,0:T(4,128)} %bitcast.17, bf16[256,4,512]{2,1,0:T(4,128)(2,1)} %x_ref.1, ...), custom_call_target="tpu_custom_call" | custom-call | tf_op jit(solution)/shard_map/layer/pallas_call | solution.py:1112
  146.9 5.3 %hand_over.1 = (f32[256,4,512]{2,1,0:T(4,128)}, f32[256,4,512]{2,1,0:T(4,128)}, f32[256,4,512]{2,1,0:T(4,128)}, f32[3,64,128]{2,1,0:T(8,128)}, f32[64,512]{1,0:T...) custom-call(f32[256,4,512]{2,1,0:T(4,128)} %get-tuple-element.29.ref, ...), custom_call_target="tpu_custom_call" | custom-call | tf_op jit(solution)/shard_map/hand_over/pallas_call | solution.py:1135

commit v5 on v4

--- a/solution.py
+++ b/solution.py
@@ -14,8 +14,9 @@
 DOCUMENTS = 4
 DOWN_DUES = (0.06, 0.35, 0.75)
 UP_DUES = (0.10, 0.5, 0.9)
-GATHER_DUE, GATHER_LEVEL, GATHER_STEP = 6, 4, 3
+GATHER_DUE, GATHER_LEVEL, GATHER_STEP = 1, 4, 4
 NEAR_DUE = 1
+GROUP = 1
 PARTS = 3
 GELU_A = 0.7978845608028654
 GELU_B = 0.044715
@@ -421,7 +422,7 @@
     xt_ref,
     o_ref,
     lse_ref,
-    results_ref,
+    base_ref,
     stage_ref,
     key_marks_ref,
     key_marks_t_ref,
@@ -514,8 +515,6 @@
 
     def next_x(slot):
         x_copy(slot).wait_send()
-        if slot + 1 < last - 1:
-            x_copy(slot + 1).start()
 
     shard_copies = [one.own_copy(local_sem.at[5 + i]) for i, one in enumerate(ffn)]
 
@@ -541,6 +540,8 @@
         x_copy(0).start()
         if last > 1:
             x_copy(last - 1).start()
+        for slot in range(1, last - 1):
+            x_copy(slot).start()
         x_col_ref[last] = home_ref[0, me // owners]
         norm_ref[...] = jnp.zeros_like(norm_ref)
         lse_columns_ref[...] = jnp.zeros_like(lse_columns_ref)
@@ -578,6 +579,7 @@
             if stage == qkv.count - 1:
                 next_x(0)
                 near_ffn.begin()
+                far_ffn[0].begin()
             qkv.advance(stage)
         for copy in shard_copies:
             copy.wait()
@@ -606,8 +608,6 @@
                 x_copy(slot).wait_recv()
             if 0 < slot < last - 1:
                 next_x(slot)
-            if turn + 1 == tensors:
-                far_ffn[0].begin()
             block = x_col_ref[slot]
             at = slice(slot * rows, (slot + 1) * rows)
             q_ref[at, :] = dot_nt(block, w_t(0)).astype(BF16) * jnp.bfloat16(0.125)
@@ -701,27 +701,44 @@
         gain_one, bias_one = norms_ref[0:1, :], norms_ref[1:2, :]
         gain_two, bias_two = norms_ref[2:3, :], norms_ref[3:4, :]
 
-        @pl.loop(0, columns)
-        def _(i):
-            column = partner_of(owners * i) // owners
-            for r in range(owners):
-
-                @pl.when(owners * i + r < last)
-                def _():
-                    mixed_copy(owners * i + r, partner_of(owners * i + r)).wait()
-
-            def slot_of(h):
-                return last - owners * (columns - 1 - i) - flip(me_low, h)
-
-            mixed = jnp.concatenate([mixed_ref[slot_of(h)] for h in range(owners)], axis=1)
-            at = pl.ds(pl.multiple_of(i * rows, rows), rows)
+        def place_of(turn):
+            first, final = 1 - (turn + columns - 1) // columns, (turn + 1) // columns
+            return turn + 1 - first - (columns - 1) * final
+
+        def slot_of(place, h):
+            return last - owners * (columns - 1 - place) - flip(me_low, h)
+
+        def mixed_at(place):
+            return jnp.concatenate([mixed_ref[slot_of(place, h)] for h in range(owners)], axis=1)
+
+        group = GROUP if columns % GROUP == 0 else 1
+
+        @pl.loop(0, columns // group)
+        def _(turn):
+            places = [place_of(turn * group + n) for n in range(group)]
+            taken = [partner_of(owners * place) // owners for place in places]
+            for place in places:
+                for r in range(owners):
+
+                    @pl.when(owners * place + r < last)
+                    def _():
+                        mixed_copy(owners * place + r, partner_of(owners * place + r)).wait()
+
+            def home(n):
+                return jnp.concatenate([home_ref[n, column] for column in taken]).astype(F32)
+
+            def replace(n, value):
+                for m, column in enumerate(taken):
+                    home_ref[n, column] = value[m * rows : (m + 1) * rows].astype(BF16)
+
+            mixed = jnp.concatenate([mixed_at(place) for place in places])
+            at = pl.ds(pl.multiple_of(turn * group * rows, group * rows), group * rows)
             branch_one = dot_nn(mixed, all_out_ref[...].reshape(width, width))
-            normed_one, factor_one = norm_forward(home_ref[0, column].astype(F32) + branch_one)
+            normed_one, factor_one = norm_forward(home(0) + branch_one)
             middle = normed_one * gain_one + bias_one
             middle_low = middle.astype(BF16)
             middle_ref[:, at] = middle_low.T
-            branch_two = jnp.zeros((rows, width), F32)
-
+            branch_two = jnp.zeros((group * rows, width), F32)
             for t in range(tensors):
                 inner = dot_nn(middle_low, all_up_ref[t].reshape(width, share))
                 square = inner * inner
@@ -733,10 +750,9 @@
                 hidden_ref[t, at, :] = hidden
                 branch_two = branch_two + dot_nn(hidden, all_down_ref[t].reshape(share, width))
             normed_two, factor_two = norm_forward(middle + branch_two)
-            results_ref[0, column] = normed_two * gain_two + bias_two
-            results_ref[1, column] = home_ref[1, column].astype(F32) + branch_one + branch_two
-            cot_dual = home_ref[3, column].astype(F32)
-            upstream = home_ref[2, column].astype(F32)
+            cot_dual, upstream = home(3), home(2)
+            replace(2, normed_two * gain_two + bias_two)
+            replace(1, home(1) + branch_one + branch_two)
             d_two = norm_backward(upstream, normed_two, factor_two, gain_two)
             norm_ref[2:3, :] += jnp.sum(upstream * normed_two, axis=0, keepdims=True)
             norm_ref[3:4, :] += jnp.sum(upstream, axis=0, keepdims=True)
@@ -751,22 +767,24 @@
             d_one = norm_backward(grad_middle, normed_one, factor_one, gain_one)
             norm_ref[0:1, :] += jnp.sum(grad_middle * normed_one, axis=0, keepdims=True)
             norm_ref[1:2, :] += jnp.sum(grad_middle, axis=0, keepdims=True)
-            results_ref[2, column] = d_one
+            for m, column in enumerate(taken):
+                base_ref[column] = d_one[m * rows : (m + 1) * rows]
             up_one = (d_one + cot_dual).astype(BF16)
             up_one_ref[:, at] = up_one.T
             grad_mixed = dot_nt(up_one, all_out_ref[...].reshape(width, width)).astype(BF16)
-            for h in range(owners):
-                slot = slot_of(h)
-                piece = grad_mixed[:, h * lanes : (h + 1) * lanes]
-
-                @pl.when(slot < last)
-                def _():
-                    stage_ref[slot, :, :lanes] = piece
-                    do_copy(slot, partner_of(slot)).start()
-
-                @pl.when(slot == last)
-                def _():
-                    do_ref[last] = piece
+            for m, place in enumerate(places):
+                for h in range(owners):
+                    slot = slot_of(place, h)
+                    piece = grad_mixed[m * rows : (m + 1) * rows, h * lanes : (h + 1) * lanes]
+
+                    @pl.when(slot < last)
+                    def _():
+                        stage_ref[slot, :, :lanes] = piece
+                        do_copy(slot, partner_of(slot)).start()
+
+                    @pl.when(slot == last)
+                    def _():
+                        do_ref[last] = piece
 
         norm_sum.begin()
         cut = (2,) * dp_bits + (width >> dp_bits,)
@@ -784,13 +802,7 @@
             g_up = dot_nn(middle_ref[...], grad_inner_ref[t]).astype(BF16)
             g_up_ref[(t,) + every + (slice(0, share),)] = g_up.reshape(cut + (share,))
 
-        def mixed_of(i):
-            def slot_of(h):
-                return last - owners * (columns - 1 - i) - flip(me_low, h)
-
-            return jnp.concatenate([mixed_ref[slot_of(h)] for h in range(owners)], axis=1)
-
-        all_mixed = jnp.concatenate([mixed_of(i) for i in range(columns)], axis=0)
+        all_mixed = jnp.concatenate([mixed_at(place_of(n)) for n in range(columns)], axis=0)
         g_out = dot_nn(up_one_ref[...], all_mixed).astype(BF16)
         for t in range(tensors):
             g_up_ref[(t,) + every + (slice(share, share + shard),)] = g_out[
@@ -801,7 +813,7 @@
     pl.run_scoped(
         forward_phase,
         pltpu.VMEM((tensors, tokens, share), BF16),
-        pltpu.VMEM((tensors, rows, share), F32),
+        pltpu.VMEM((tensors, GROUP * rows, share), F32),
         pltpu.VMEM((tensors, tokens, share), BF16),
         pltpu.VMEM((width, tokens), BF16),
         pltpu.VMEM((width, tokens), BF16),
@@ -911,7 +923,7 @@
                 stage_ref[wave] = part.astype(BF16)
                 input_copy(wave, partner_of(wave)).start()
             else:
-                results_ref[2, me // owners] += part
+                base_ref[me // owners] += part
 
         for i in range(3):
             g = dot_nn(xt_ref[...], grads_ref[i]).astype(BF16)
@@ -941,7 +953,8 @@
         ]
 
         def store(n):
-            turned_ref[n] = jnp.swapaxes(results_ref[n], 0, 1)
+            made = base_ref[...].astype(BF16) if n == 2 else home_ref[2 - n]
+            turned_ref[n] = jnp.swapaxes(made, 0, 1)
             stores[n].start()
 
         def advance(step):
@@ -957,7 +970,7 @@
             x_copy(last - 1).wait_send()
         for slot in range(last):
             input_copy(slot, partner_of(slot)).wait()
-            results_ref[2, partner_of(slot) // owners] += input_land_ref[slot].astype(F32)
+            base_ref[partner_of(slot) // owners] += input_land_ref[slot].astype(F32)
         store(2)
         for step in range(2, dp_bits):
             advance(step)
@@ -979,13 +992,13 @@
         for copy in stores:
             copy.wait()
 
-    pl.run_scoped(end_phase, pltpu.VMEM((3, rows, columns, width), F32))
+    pl.run_scoped(end_phase, pltpu.VMEM((3, rows, columns, width), BF16))
 
 
 def hand_over_kernel(*refs):
     sources, results = refs[:7], refs[7:]
     for n in range(3):
-        results[n][...] = sources[n][...]
+        results[n][...] = sources[n][...].astype(F32)
 
     @pl.when(pl.program_id(0) == 0)
     def _():
@@ -1052,9 +1065,9 @@
     layer = pl.pallas_call(
         functools.partial(layer_kernel, dp_bits, columns),
         out_shape=(
-            shape((rows, columns, width), F32),
-            shape((rows, columns, width), F32),
-            shape((rows, columns, width), F32),
+            shape((rows, columns, width), BF16),
+            shape((rows, columns, width), BF16),
+            shape((rows, columns, width), BF16),
         )
         + small_out,
         in_specs=[in_place] * 13,
@@ -1088,7 +1101,7 @@
             pltpu.VMEM((width, length), BF16),
             pltpu.VMEM((tensors, rows, lanes), F32),
             pltpu.VMEM((tensors, max(heads, 8), rows), F32),
-            pltpu.VMEM((3, columns, rows, width), F32),
+            pltpu.VMEM((columns, rows, width), F32),
             pltpu.VMEM((tensors - 1, rows, width), BF16),
             pltpu.VMEM((length, 2 * E), BF16),
             pltpu.VMEM((2 * E, length), BF16),

time: 152 us -> 148 us (0.974)
  Pallas kernels: 151 us -> 147 us
    pallas_call x1, Pallas kernels: 146 us -> 142 us  [body(): layer(segment_ids.T, x_post, x_dual, cot_post, cot_dual, w_qkv, *shards,...]
where the time goes in v5:
time: 148 us
  Pallas kernels  147 us (99%)
    pallas_call x1, Pallas kernels, body(): layer(segment_ids.T, x_post, x_dual, cot_post, cot_dual, w_qkv, *shards,...  142 us
    pallas_call x1, Pallas kernels, body(): pl.pallas_call(hand_over_kernel, out_shape=tuple((shape(one.shape, F32) f...  4.67 us

profile of v5, /device:TPU:0, one launch (start us, length us, event | category | flops | bytes accessed | tf_op | source)
XLA Modules:
  0.0 148.0 jit_solution(12366371208151308389)
XLA Ops:
  0.6 142.5 %layer.1 = (bf16[256,4,512]{2,1,0:T(4,128)(2,1)}, bf16[256,4,512]{2,1,0:T(4,128)(2,1)}, bf16[256,4,512]{2,1,0:T(4,128)(2,1)}, f32[3,64,128]{2,1,0:T(8,128)}, f32...) custom-call(s32[4,1024]{1,0:T(4,128)} %bitcast.17, bf16[256,4,512]{2,1,0:T(4,128)(2,1)} %x_ref.1, ...), custom_call_target="tpu_custom_call" | custom-call | tf_op jit(solution)/shard_map/layer/pallas_call | solution.py:1125
  143.1 4.7 %hand_over.1 = (f32[256,4,512]{2,1,0:T(4,128)}, f32[256,4,512]{2,1,0:T(4,128)}, f32[256,4,512]{2,1,0:T(4,128)}, f32[3,64,128]{2,1,0:T(8,128)}, f32[64,512]{1,0:T...) custom-call(bf16[256,4,512]{2,1,0:T(4,128)(2,1)} %get-tuple-element., ...), custom_call_target="tpu_custom_call" | custom-call | tf_op jit(solution)/shard_map/hand_over/pallas_call | solution.py:1148

commit v6 on v5

--- a/solution.py
+++ b/solution.py
@@ -16,6 +16,7 @@
 UP_DUES = (0.10, 0.5, 0.9)
 GATHER_DUE, GATHER_LEVEL, GATHER_STEP = 1, 4, 4
 NEAR_DUE = 1
+CHUNKS = 2
 GROUP = 1
 PARTS = 3
 GELU_A = 0.7978845608028654
@@ -322,7 +323,7 @@
                 for spot in itertools.product((0, 1), repeat=len(land.shape) - 3):
                     whole = (t,) + spot[:place] + (own,) + spot[place:]
                     here = (t,) + spot
-                    land[here] = (land[here].astype(F32) + source[whole].astype(F32)).astype(BF16)
+                    land[here] = land[here] + source[whole]
 
         if step >= len(self.lands):
             for mask, place in self.joins[step - len(self.lands)]:
@@ -528,8 +529,8 @@
             pltpu.make_async_copy(ref, norms_ref.at[pl.ds(n, 1)], local_sem.at[9 + n])
             for n, ref in enumerate((gain_one_ref, bias_one_ref, gain_two_ref, bias_two_ref))
         ]
+        greet(dp_bits, tensors)
         start(loads[:1] + [load_qkv] + loads[1:] + small_loads + shard_copies)
-        greet(dp_bits, tensors)
         load_qkv.wait()
         for i in range(3):
             all_qkv_ref[me, i] = raw_qkv_ref[i].T.reshape(all_qkv_ref.shape[2:])
@@ -537,10 +538,7 @@
         home_ref[0] = jnp.swapaxes(raw_ref[0], 0, 1)
         greeted(dp_bits, tensors)
         qkv.begin()
-        x_copy(0).start()
-        if last > 1:
-            x_copy(last - 1).start()
-        for slot in range(1, last - 1):
+        for slot in ([last - 1] if last > 1 else []) + list(range(max(last - 1, 1))):
             x_copy(slot).start()
         x_col_ref[last] = home_ref[0, me // owners]
         norm_ref[...] = jnp.zeros_like(norm_ref)
@@ -668,10 +666,14 @@
                 for half in range(2):
                     own = (lane < E) if half == 0 else (lane >= E)
                     own_queries = jnp.where(own, queries, jnp.zeros_like(queries))
-                    scores = dot_nn(jnp.concatenate([own_queries, marks], axis=1), keys)
-                    top = jnp.max(scores, axis=1, keepdims=True)
-                    raised = jnp.exp(scores - top).astype(BF16)
-                    result = dot_nn(raised, values)
+                    marked = jnp.concatenate([own_queries, marks], axis=1)
+                    tops, sums = [], []
+                    part = rows // CHUNKS
+                    for n in range(CHUNKS):
+                        scores = dot_nn(marked[n * part : (n + 1) * part], keys)
+                        tops.append(jnp.max(scores, axis=1, keepdims=True))
+                        sums.append(dot_nn(jnp.exp(scores - tops[-1]).astype(BF16), values))
+                    top, result = jnp.concatenate(tops), jnp.concatenate(sums)
                     denom = result[:, 2 * E + DOCUMENTS : 2 * E + DOCUMENTS + 1]
                     results.append(result[:, : 2 * E] * (1.0 / denom))
                     lse = top + jnp.log(denom)

time: 148 us -> 147 us (level)
  no operation moved by 1% of the time
where the time goes in v6:
time: 147 us
  Pallas kernels  146 us (99%)
    pallas_call x1, Pallas kernels, body(): layer(segment_ids.T, x_post, x_dual, cot_post, cot_dual, w_qkv, *shards,...  142 us
    pallas_call x1, Pallas kernels, body(): pl.pallas_call(hand_over_kernel, out_shape=tuple((shape(one.shape, F32) f...  4.67 us

profile of v6, /device:TPU:0, one launch (start us, length us, event | category | flops | bytes accessed | tf_op | source)
XLA Modules:
  0.0 147.2 jit_solution(955015863780056512)
XLA Ops:
  0.6 141.7 %layer.1 = (bf16[256,4,512]{2,1,0:T(4,128)(2,1)}, bf16[256,4,512]{2,1,0:T(4,128)(2,1)}, bf16[256,4,512]{2,1,0:T(4,128)(2,1)}, f32[3,64,128]{2,1,0:T(8,128)}, f32...) custom-call(s32[4,1024]{1,0:T(4,128)} %bitcast.17, bf16[256,4,512]{2,1,0:T(4,128)(2,1)} %x_ref.1, ...), custom_call_target="tpu_custom_call" | custom-call | tf_op jit(solution)/shard_map/layer/pallas_call | solution.py:1127
  142.3 4.7 %hand_over.1 = (f32[256,4,512]{2,1,0:T(4,128)}, f32[256,4,512]{2,1,0:T(4,128)}, f32[256,4,512]{2,1,0:T(4,128)}, f32[3,64,128]{2,1,0:T(8,128)}, f32[64,512]{1,0:T...) custom-call(bf16[256,4,512]{2,1,0:T(4,128)(2,1)} %get-tuple-element., ...), custom_call_target="tpu_custom_call" | custom-call | tf_op jit(solution)/shard_map/hand_over/pallas_call | solution.py:1150
